TPU v7x, 256 devices: a whole 4x4x8 slice. The times are simulated.
256 devices in a mesh: grp: 2 (over core), gx: 32 (over z, x), gy: 4 (over y).
Axes of the slice: x: 4, y: 4, z: 8, core: 2. Of those that a mesh axis runs over, the one named last changes fastest.
Arguments:
- section_levels: bfloat16 [2, 10, 1024, 128, 128], P('grp', None, 'gx', 'gy'), may hold values from -6 to 6
- to_cells: bfloat16 [256, 32, 4, 16], P('gx', 'gy'), may hold values from -1.5 to 1.5
- to_nodes: bfloat16 [256, 32, 16, 4], P('gx', 'gy'), may hold values from -3 to 3
- owner_map: int32 [32, 4, 64, 1], P('gx', 'gy'), may hold values from 0 to 127; in each aligned block of 64 rows (0 to 63, 64 to 127, ..., all dimensions but the last counted through in order) at most 2 rows name the same one
- forcing: float32 [32, 4, 8, 4, 256], P('gx', 'gy'), may hold values from -6 to 6
- vertical_map: float32 [128, 128], replicated, may hold values from -0.5 to 0.5
- coupling: float32 [8, 10], replicated, may hold values from -2 to 2
- relaxation: float32 [8, 128], replicated, may hold values from 0.2 to 2
Outputs:
- new_state: bfloat16 [10, 1024, 128, 128], P(None, 'gx', 'gy', 'grp')
Inputs may be any that keep to these rules, and one draw needn't show every extreme that they name: `owner_map`: no physics owner receives more than 2 elements from the elements of one device, and some owner receives exactly 2 from some device.
All inputs are finite; a program needn't handle non-finite values.
Results may differ from a plain program's by a relative error of at most 0.0051.
Values may be sent and summed in bfloat16 or wider, within the bound.
A program may use at most 128 MiB of HBM per device.

v0:
```python
import jax
import jax.numpy as jnp
import numpy as np
from jax import lax
from jax.sharding import PartitionSpec as P

dt_dynamics = 0.1
dt_physics = 0.25
highest = lax.Precision.HIGHEST


def with_halo(cells, sides, width):
    for axis, dim in sides:
        count = lax.axis_size(axis)
        head = lax.slice_in_dim(cells, 0, width, axis=dim)
        tail = lax.slice_in_dim(cells, cells.shape[dim] - width, cells.shape[dim], axis=dim)
        cells = jnp.concatenate(
            [
                lax.ppermute(tail, axis, [(i, (i + 1) % count) for i in range(count)]),
                cells,
                lax.ppermute(head, axis, [((i + 1) % count, i) for i in range(count)]),
            ],
            axis=dim,
        )
    return cells


def from_partner(shard, axis, bit):
    return lax.ppermute(shard, axis, [(i, i ^ 1 << bit) for i in range(lax.axis_size(axis))])


def gll_derivative():
    points = np.array([-1.0, -1.0 / np.sqrt(5.0), 1.0 / np.sqrt(5.0), 1.0])
    barycentric = np.ones(4)
    for first in range(4):
        for second in range(4):
            if first != second:
                barycentric[first] = barycentric[first] / (points[first] - points[second])
    matrix = np.zeros((4, 4))
    for first in range(4):
        for second in range(4):
            if first != second:
                matrix[first, second] = (
                    barycentric[second] / barycentric[first] / (points[first] - points[second])
                )
        matrix[first, first] = -np.sum(matrix[first])
    return jnp.asarray(matrix, jnp.float32)


def derivatives(field):
    derivative = gll_derivative()
    full_shape = field.shape
    lead_dims = full_shape[:-3]
    extent_x, extent_y, levels = full_shape[-3:]
    blocks = field.reshape(lead_dims + (extent_x // 4, 4, extent_y, levels))
    along_x = jnp.einsum("ij,...ejyl->...eiyl", derivative, blocks, precision=highest).reshape(
        full_shape
    )
    blocks = field.reshape(lead_dims + (extent_x, extent_y // 4, 4, levels))
    along_y = jnp.einsum("ij,...xejl->...xeil", derivative, blocks, precision=highest).reshape(
        full_shape
    )
    return (along_x, along_y)


def edge_average(center, lower_side, upper_side, axis):
    position = lax.broadcasted_iota(jnp.int32, center.shape, axis) % 4
    upper_mean = 0.5 * (center + upper_side)
    lower_mean = 0.5 * (center + lower_side)
    return jnp.where(position == 3, upper_mean, jnp.where(position == 0, lower_mean, center))


def column_physics(cells, local_forcing, vertical_map, coupling, relaxation):
    ntend = coupling.shape[0]
    mixed = jnp.einsum("sfpl,lm->sfpm", cells, vertical_map, precision=highest)
    response = jnp.einsum("gf,sfpl->sgpl", coupling, jnp.tanh(mixed), precision=highest)
    damping = relaxation[None, :, None, :] * (cells[:, :ntend] - mixed[:, :ntend])
    tendency = response - damping + local_forcing[..., None]
    return tendency.astype(jnp.bfloat16)


def pack_rows(values, sources):
    padding = jnp.zeros((1,) + values.shape[1:], values.dtype)
    return jnp.take(jnp.concatenate([values, padding], axis=0), sources, axis=0)


def shards(
    section_levels, to_cells, to_nodes, owner_map, forcing, vertical_map, coupling, relaxation
):
    member = lax.axis_index("grp")
    current = section_levels[0]
    fields, extent_x, extent_y, levels = current.shape
    field = current.astype(jnp.float32)
    along_x, along_y = derivatives(field)
    tendency = -(field[0] * along_x + field[1] * along_y)
    padded = with_halo(tendency, (("gx", 1),), 1)
    tendency = edge_average(tendency, padded[:, :-2], padded[:, 2:], 1)
    padded = with_halo(tendency, (("gy", 2),), 1)
    tendency = edge_average(tendency, padded[:, :, :-2], padded[:, :, 2:], 2)
    rounded = tendency.astype(jnp.bfloat16)
    outgoing = jnp.where(member == 0, rounded, current)
    incoming = from_partner(outgoing, "grp", 0)
    initial = jnp.where(member == 0, incoming, current)
    section_rate = jnp.where(member == 0, rounded, incoming)
    advanced = (
        initial.astype(jnp.float32) + dt_dynamics * section_rate.astype(jnp.float32)
    ).astype(jnp.bfloat16)
    elems_x = to_cells.shape[0]
    elems_y = to_cells.shape[1]
    element_count = elems_x * elems_y
    peer_count = lax.axis_size(("gx", "gy"))
    capacity = max(2, 2 * element_count // peer_count)
    owners = owner_map.reshape(element_count)
    onehot = (owners[:, None] == jnp.arange(peer_count, dtype=jnp.int32)[None, :]).astype(jnp.int32)
    rank = jnp.sum((jnp.cumsum(onehot, axis=0) - onehot) * onehot, axis=1)
    slots = owners * capacity + rank
    sources = jnp.full((peer_count * capacity,), element_count, jnp.int32)
    sources = sources.at[slots].set(jnp.arange(element_count, dtype=jnp.int32))
    nodes = advanced.reshape(fields, elems_x, 4, elems_y, 4, levels).transpose(1, 3, 0, 2, 4, 5)
    nodes = nodes.reshape(element_count, fields, 16, levels)
    weights_in = to_cells.reshape(element_count, 4, 16)
    sent_nodes, sent_weights = (
        lax.all_to_all(
            pack_rows(nodes, sources), ("gx", "gy"), split_axis=0, concat_axis=0, tiled=True
        ),
        lax.all_to_all(
            pack_rows(weights_in, sources), ("gx", "gy"), split_axis=0, concat_axis=0, tiled=True
        ),
    )
    cells = jnp.einsum(
        "spn,sfnl->sfpl", sent_weights, sent_nodes, preferred_element_type=jnp.float32
    )
    local_forcing = forcing[0, 0].transpose(2, 0, 1)
    column_tend = column_physics(cells, local_forcing, vertical_map, coupling, relaxation)
    returned = lax.all_to_all(column_tend, ("gx", "gy"), split_axis=0, concat_axis=0, tiled=True)
    element_tend = jnp.take(returned, slots, axis=0)
    ntend = element_tend.shape[1]
    weights_out = to_nodes.reshape(element_count, 16, 4)
    nodal = jnp.einsum(
        "enp,egpl->egnl", weights_out, element_tend, preferred_element_type=jnp.float32
    )
    nodal = nodal.reshape(elems_x, elems_y, ntend, 4, 4, levels).transpose(2, 0, 3, 1, 4, 5)
    nodal = nodal.reshape(ntend, extent_x, extent_y, levels)
    updated = advanced[:ntend].astype(jnp.float32) + dt_physics * nodal
    result = jnp.concatenate([updated.astype(jnp.bfloat16), advanced[ntend:]], axis=0)
    half_levels = levels // 2
    return lax.dynamic_slice_in_dim(result, member * half_levels, half_levels, 3)


def solution(mesh):
    in_specs = (
        P("grp", None, "gx", "gy", None),
        P("gx", "gy", None, None),
        P("gx", "gy", None, None),
        P("gx", "gy", None, None),
        P("gx", "gy", None, None, None),
        P(),
        P(),
        P(),
    )
    out_specs = P(None, "gx", "gy", "grp")
    return jax.shard_map(shards, mesh=mesh, in_specs=in_specs, out_specs=out_specs, check_vma=False)
```

profile of v0, /device:TPU:32, one launch (start us, length us, event | category | flops | bytes accessed | tf_op | source)
XLA Modules:
  0.0 444.0 jit_solution(2528026238028132281)
XLA Ops:
  0.0 2.6 bitcast_convert_fusion
  2.7 4.4 fusion.23
  7.8 4.4 fusion.41
  13.8 2.4 collective-permute-start
  16.1 3.6 collective-permute-done
  19.8 4.1 collective-permute-done.1
  23.9 4.1 fusion.12
  29.9 3.1 collective-permute-start.2
  33.2 2.6 collective-permute-done.2
  35.9 3.8 collective-permute-done.3
  39.7 9.9 %bitcast_select_fusion.1 = (bf16[10,32,32,128]{3,2,1,0:T(8,128)(2,1)}, bf16[10,32,32,128]{3,2,1,0:T(8,128)(2,1)}) fusion(bf16[1,10,32,32,128]{4,3,2,1,0:T(8,128)(2,1)S(1)} %copy-done.1, pred[]{:T(512)S(6)} %eq.33, f32[10,32,32,128]{3,2,1,0:T(8,128)} %fusion.12, f32[10,32,1,128]{3,2,1,0:T(1,128)S(1)} %collective-permute-done.3, ...), kind=kLoop, calls=%fused_computation.40 | loop fusion | flops 17039360 | bytes 13435169 | tf_op jit(solution)/shard_map/jit(_where)/select_n | solution.py:101
  52.9 12.3 %all-to-all-start.1 = ((bf16[256,4,16]{2,1,0:T(4,128)(2,1)}), bf16[256,4,16]{2,1,0:T(4,128)(2,1)S(1)}, u32[]{:S(2)}, u32[]{:S(2)}) async-start(bf16[256,4,16]{2,1,0:T(4,128)(2,1)} %broadcast_select_fusion.1), calls=%async_computation.1 | async-start | bytes 524288 | tf_op jit(solution)/shard_map/all_to_all | solution.py:126
  65.2 3.9 add_convert_fusion
  72.0 9.3 %gather_fusion = bf16[256,10,16,128]{3,2,1,0:T(8,128)(2,1)} fusion(bf16[65,10,16,128]{3,2,1,0:T(8,128)(2,1)S(1)} %concatenate.27, s32[1024]{0:T(1024)S(1)} %pad_clamp_fusion.1), kind=kCustom, calls=%fused_computation | custom fusion | bytes 20972544 | tf_op jit(solution)/shard_map/jit(_take)/gather | solution.py:84
  81.4 10.1 %broadcast_select_fusion = bf16[256,10,16,128]{3,2,1,0:T(8,128)(2,1)} fusion(bf16[256,10,16,128]{3,2,1,0:T(8,128)(2,1)} %gather_fusion, pred[256]{0:T(512)(128)(4,1)S(1)} %compare_and_fusion), kind=kLoop, calls=%fused_computation.4 | loop fusion | flops 5242880 | bytes 20971776 | tf_op jit(solution)/shard_map/jit(_take)/select_n | solution.py:84
  91.5 14.7 %all-to-all-start = ((bf16[256,10,16,128]{3,2,1,0:T(8,128)(2,1)}), bf16[256,10,16,128]{3,2,1,0:T(8,128)(2,1)}, u32[]{:S(2)}, u32[]{:S(2)}) async-start(bf16[256,10,16,128]{3,2,1,0:T(8,128)(2,1)} %broadcast_select_fusion), calls=%async_computation | async-start | bytes 20971520 | tf_op jit(solution)/shard_map/all_to_all | solution.py:123
  107.6 227.0 %all-to-all-done = bf16[256,10,16,128]{3,2,1,0:T(8,128)(2,1)} async-done(((bf16[256,10,16,128]{3,2,1,0:T(8,128)(2,1)}), bf16[256,10,16,128]{3,2,1,0:T(8,128)(2,1)}, u32[]{:S(2)}, u32[]{:S(2)}) %all-to-all-start) | async-done | bytes 10485792 | tf_op jit(solution)/shard_map/all_to_all | solution.py:123
  334.6 7.8 %convolution_bitcast_fusion = f32[256,10,4,128]{3,2,1,0:T(4,128)} fusion(bf16[256,10,16,128]{3,2,1,0:T(8,128)(2,1)} %all-to-all-done, bf16[256,4,16]{2,1,0:T(4,128)(2,1)S(1)} %all-to-all-done.1), kind=kOutput, calls=%fused_computation.45 | convolution fusion | flops 41943040 | bytes 15761408 | tf_op jit(solution)/shard_map/spn,sfnl->sfpl/dot_general | solution.py:130
  342.4 7.2 %fusion.40 = (f32[256,10,4,128]{3,0,2,1:T(8,128)S(1)}, f32[256,10,4,128]{3,0,2,1:T(8,128)S(1)}) fusion(f32[128,128]{1,0:T(8,128)S(1)} %copy-done, f32[256,10,4,128]{3,2,1,0:T(4,128)} %convolution_bitcast_fusion), kind=kOutput, calls=%fused_computation.76 | convolution fusion | flops 2013265920 | bytes 15794176 | tf_op jit(solution)/shard_map/sfpl,lm->sfpm/dot_general | solution.py:75
  350.3 10.9 %fusion = f32[256,4,128,8]{2,3,1,0:T(8,128)S(1)} fusion(f32[256,10,4,128]{3,0,2,1:T(8,128)S(1)} %get-tuple-element.13, f32[8,10]{1,0:T(8,128)S(1)} %copy-done.10), kind=kOutput, calls=%fused_computation.5 | convolution fusion | flops 125829120 | bytes 9437504 | tf_op jit(solution)/shard_map/gf,sfpl->sgpl/dot_general | solution.py:76
  361.2 9.3 %fusion.20 = bf16[256,8,4,128]{3,2,1,0:T(4,128)(2,1)} fusion(f32[256,10,4,128]{3,2,1,0:T(4,128)S(1)} %bitcast.79, f32[256,8,4,128]{3,0,2,1:T(8,128)S(1)} %slice.74, f32[256,4,128,8]{2,3,1,0:T(8,128)S(1)} %fusion, f32[256,8,4]{2,1,0:T(8,128)S(1)} %copy-done.4, f32[8,128]{1,0:T(8,128)S(1)} %copy-done.11), kind=kLoop, calls=%fused_computation.36 | loop fusion | flops 5242880 | bytes 14716928 | tf_op jit(solution)/shard_map/convert_element_type | solution.py:79
  370.6 11.9 %all-to-all-start.2 = ((bf16[256,8,4,128]{3,2,1,0:T(4,128)(2,1)}), bf16[256,8,4,128]{3,2,1,0:T(4,128)(2,1)}, u32[]{:S(2)}, u32[]{:S(2)}) async-start(bf16[256,8,4,128]{3,2,1,0:T(4,128)(2,1)} %fusion.20), calls=%async_computation.2 | async-start | bytes 4194304 | tf_op jit(solution)/shard_map/all_to_all | solution.py:135
  383.4 52.3 %all-to-all-done.2 = bf16[256,8,4,128]{3,2,1,0:T(4,128)(2,1)} async-done(((bf16[256,8,4,128]{3,2,1,0:T(4,128)(2,1)}), bf16[256,8,4,128]{3,2,1,0:T(4,128)(2,1)}, u32[]{:S(2)}, u32[]{:S(2)}) %all-to-all-start.2) | async-done | bytes 2097184 | tf_op jit(solution)/shard_map/all_to_all | solution.py:135
  435.7 2.6 gather_fusion.2
  (67 shorter events, 18.7 us)
Async XLA Ops:
  0.0 342.4 %copy-start = (f32[128,128]{1,0:T(8,128)S(1)}, f32[128,128]{1,0:T(8,128)}, u32[]{:S(2)}) copy-start(f32[128,128]{1,0:T(8,128)} %param.14) | copy-start | bytes 196612
  0.0 2.7 copy-start.9
  0.0 2.7 copy-start.1
  13.8 6.0 %collective-permute-start = (f32[10,1,32,128]{3,2,1,0:T(8,128)S(1)}, f32[10,1,32,128]{3,2,1,0:T(8,128)S(1)}, u32[]{:S(2)}, u32[]{:S(2)}) collective-permute-start(f32[10,1,32,128]{3,2,1,0:T(8,128)S(1)} %get-tuple-element.9), channel_id=1, source_target_pairs={{4,0},{8,4},{12,8},{16,12},{20,16},{24,20},{28,24},{32,28},{36,32}... | collective-permute-start | bytes 491528 | tf_op jit(solution)/shard_map/ppermute | solution.py:21
  16.1 7.8 %collective-permute-start.1 = (f32[10,1,32,128]{3,2,1,0:T(8,128)S(1)}, f32[10,1,32,128]{3,2,1,0:T(8,128)S(1)}, u32[]{:S(2)}, u32[]{:S(2)}) collective-permute-start(f32[10,1,32,128]{3,2,1,0:T(8,128)S(1)} %get-tuple-element.10), channel_id=1, source_target_pairs={{0,4},{4,8},{8,12},{12,16},{16,20},{20,24},{24,28},{28,32},{32,36}... | collective-permute-start | bytes 491528 | tf_op jit(solution)/shard_map/ppermute | solution.py:19
  29.9 5.9 %collective-permute-start.2 = (f32[10,32,1,128]{3,2,1,0:T(1,128)S(1)}, f32[10,32,1,128]{3,2,1,0:T(1,128)S(1)}, u32[]{:S(2)}, u32[]{:S(2)}) collective-permute-start(f32[10,32,1,128]{3,2,1,0:T(1,128)S(1)} %get-tuple-element.7), channel_id=1, source_target_pairs={{1,0},{2,1},{3,2},{0,3},{5,4},{6,5},{7,6},{4,7},{9,8},{10,9},{11,1... | collective-permute-start | bytes 491528 | tf_op jit(solution)/shard_map/ppermute | solution.py:21
  33.0 6.7 %collective-permute-start.3 = (f32[10,32,1,128]{3,2,1,0:T(1,128)S(1)}, f32[10,32,1,128]{3,2,1,0:T(1,128)S(1)}, u32[]{:S(2)}, u32[]{:S(2)}) collective-permute-start(f32[10,32,1,128]{3,2,1,0:T(1,128)S(1)} %get-tuple-element.8), channel_id=1, source_target_pairs={{0,1},{1,2},{2,3},{3,0},{4,5},{5,6},{6,7},{7,4},{8,9},{9,10},{10,1... | collective-permute-start | bytes 491528 | tf_op jit(solution)/shard_map/ppermute | solution.py:19
  33.2 16.4 %copy-start.12 = (s32[1,1,64,1]{2,3,1,0:T(1,128)S(1)}, s32[1,1,64,1]{2,3,1,0:T(1,128)}, u32[]{:S(2)}) copy-start(s32[1,1,64,1]{2,3,1,0:T(1,128)} %param.12) | copy-start | bytes 772
  33.2 16.6 %copy-start.7 = (bf16[8,8,4,16]{3,2,1,0:T(4,128)(2,1)S(1)}, bf16[8,8,4,16]{3,2,1,0:T(4,128)(2,1)}, u32[]{:S(2)}) copy-start(bf16[8,8,4,16]{3,2,1,0:T(4,128)(2,1)} %param.10) | copy-start | bytes 24580
  49.6 15.6 %collective-permute-start.4 = (bf16[10,32,32,128]{3,2,1,0:T(8,128)(2,1)}, bf16[10,32,32,128]{3,2,1,0:T(8,128)(2,1)}, u32[]{:S(2)}, u32[]{:S(2)}) collective-permute-start(bf16[10,32,32,128]{3,2,1,0:T(8,128)(2,1)} %get-tuple-element.5), channel_id=1, source_target_pairs={{0,128},{128,0},{1,129},{129,1},{2,130},{130,2},{3,131},{131,3},{4... | collective-permute-start | bytes 7864328 | tf_op jit(solution)/shard_map/ppermute | solution.py:29
  52.9 38.6 %all-to-all-start.1 = ((bf16[256,4,16]{2,1,0:T(4,128)(2,1)}), bf16[256,4,16]{2,1,0:T(4,128)(2,1)S(1)}, u32[]{:S(2)}, u32[]{:S(2)}) async-start(bf16[256,4,16]{2,1,0:T(4,128)(2,1)} %broadcast_select_fusion.1), calls=%async_computation.1 | async-start | bytes 524288 | tf_op jit(solution)/shard_map/all_to_all | solution.py:126
  69.1 2.4 copy-start.2
  91.5 14.7 %copy-start.8 = (f32[1,1,8,4,256]{4,3,2,1,0:T(4,128)S(1)}, f32[1,1,8,4,256]{4,3,2,1,0:T(4,128)}, u32[]{:S(2)}) copy-start(f32[1,1,8,4,256]{4,3,2,1,0:T(4,128)} %param.13) | copy-start | bytes 98308
  91.5 243.1 %all-to-all-start = ((bf16[256,10,16,128]{3,2,1,0:T(8,128)(2,1)}), bf16[256,10,16,128]{3,2,1,0:T(8,128)(2,1)}, u32[]{:S(2)}, u32[]{:S(2)}) async-start(bf16[256,10,16,128]{3,2,1,0:T(8,128)(2,1)} %broadcast_select_fusion), calls=%async_computation | async-start | bytes 20971520 | tf_op jit(solution)/shard_map/all_to_all | solution.py:123
  349.6 0.7 copy-start.10
  349.6 11.6 %slice-start = ((s8[5242880]{0:T(1024)(128)(4,1)}), s8[1048576]{0:T(1024)(128)(4,1)S(1)}, s32[]{:S(2)}) async-start(s8[5242880]{0:T(1024)(128)(4,1)} %bitcast.78), calls=%async_computation.3 | async-start | bytes 2097152
  350.3 10.9 %slice-start.1 = ((s8[5242880]{0:T(1024)(128)(4,1)}), s8[4194304]{0:T(1024)(128)(4,1)S(1)}, s32[]{:S(2)}) async-start(s8[5242880]{0:T(1024)(128)(4,1)} %bitcast.78), calls=%async_computation.4 | async-start | bytes 8388608
  350.3 10.9 %copy-start.4 = (f32[256,8,4]{2,1,0:T(8,128)S(1)}, f32[256,8,4]{2,1,0:T(8,128)}, u32[]{:S(2)}) copy-start(f32[256,8,4]{2,1,0:T(8,128)} %copy.30) | copy-start | bytes 98308
  350.3 10.9 %copy-start.11 = (f32[8,128]{1,0:T(8,128)S(1)}, f32[8,128]{1,0:T(8,128)}, u32[]{:S(2)}) copy-start(f32[8,128]{1,0:T(8,128)} %param.16) | copy-start | bytes 12292
  361.2 21.3 %copy-start.3 = (bf16[10,32,32,128]{3,2,1,0:T(8,128)(2,1)S(1)}, bf16[10,32,32,128]{3,2,1,0:T(8,128)(2,1)}, u32[]{:S(2)}) copy-start(bf16[10,32,32,128]{3,2,1,0:T(8,128)(2,1)} %copy-done.2) | copy-start | bytes 7864324
  370.6 67.7 %copy-start.6 = (bf16[8,8,16,4]{2,3,1,0:T(4,128)(2,1)S(1)}, bf16[8,8,16,4]{2,3,1,0:T(4,128)(2,1)}, u32[]{:S(2)}) copy-start(bf16[8,8,16,4]{2,3,1,0:T(4,128)(2,1)} %param.11) | copy-start | bytes 24580
  370.6 65.1 %all-to-all-start.2 = ((bf16[256,8,4,128]{3,2,1,0:T(4,128)(2,1)}), bf16[256,8,4,128]{3,2,1,0:T(4,128)(2,1)}, u32[]{:S(2)}, u32[]{:S(2)}) async-start(bf16[256,8,4,128]{3,2,1,0:T(4,128)(2,1)} %fusion.20), calls=%async_computation.2 | async-start | bytes 4194304 | tf_op jit(solution)/shard_map/all_to_all | solution.py:135
  440.3 1.0 copy-start.5
where the time goes:
time: 453 us; the launch traced here: 444 us
  waiting for transfers between devices  294 us (65%)
  other arithmetic  45.7 us (10%)
  starting transfers between devices  44.6 us (10%)
  matrix products  35.5 us (8%)
  local copies, waits for them, and re-layouts  23.8 us (5%)
    all_to_all x1, waiting for transfers between devices, shards(): lax.all_to_all(pack_rows(nodes, sources), ('gx', 'gy'), split_axis=0, con...  227 us
    all_to_all x1, waiting for transfers between devices, shards(): lax.all_to_all(column_tend, ('gx', 'gy'), split_axis=0, concat_axis=0, ti...  52.3 us
    all_to_all x1, starting transfers between devices, shards(): lax.all_to_all(pack_rows(nodes, sources), ('gx', 'gy'), split_axis=0, con...  14.7 us
    all_to_all x1, starting transfers between devices, shards(): lax.all_to_all(pack_rows(weights_in, sources), ('gx', 'gy'), split_axis=0...  12.3 us
    all_to_all x1, starting transfers between devices, shards(): lax.all_to_all(column_tend, ('gx', 'gy'), split_axis=0, concat_axis=0, ti...  11.9 us
    select_n x3, other arithmetic, pack_rows(): return jnp.take(jnp.concatenate([values, padding], axis=0), sources, axis=0)  11.2 us
    dot_general x1, matrix products, column_physics(): jnp.einsum('gf,sfpl->sgpl', coupling, jnp.tanh(mixed), precision=highest)  10.9 us
    gather x2, local copies, waits for them, and re-layouts, pack_rows(): return jnp.take(jnp.concatenate([values, padding], axis=0), sources, axis=0)  10.3 us
  transfers between devices with their start and end apart: 8, of which 6 were waited for; matrix products, arithmetic and copies ran while one was open for 7% of the time, Pallas kernels for 0%

commit v1 on v0

--- a/solution.py
+++ b/solution.py
@@ -70,20 +70,6 @@
     return jnp.where(position == 3, upper_mean, jnp.where(position == 0, lower_mean, center))
 
 
-def column_physics(cells, local_forcing, vertical_map, coupling, relaxation):
-    ntend = coupling.shape[0]
-    mixed = jnp.einsum("sfpl,lm->sfpm", cells, vertical_map, precision=highest)
-    response = jnp.einsum("gf,sfpl->sgpl", coupling, jnp.tanh(mixed), precision=highest)
-    damping = relaxation[None, :, None, :] * (cells[:, :ntend] - mixed[:, :ntend])
-    tendency = response - damping + local_forcing[..., None]
-    return tendency.astype(jnp.bfloat16)
-
-
-def pack_rows(values, sources):
-    padding = jnp.zeros((1,) + values.shape[1:], values.dtype)
-    return jnp.take(jnp.concatenate([values, padding], axis=0), sources, axis=0)
-
-
 def shards(
     section_levels, to_cells, to_nodes, owner_map, forcing, vertical_map, coupling, relaxation
 ):
@@ -109,42 +95,45 @@
     elems_y = to_cells.shape[1]
     element_count = elems_x * elems_y
     peer_count = lax.axis_size(("gx", "gy"))
-    capacity = max(2, 2 * element_count // peer_count)
     owners = owner_map.reshape(element_count)
-    onehot = (owners[:, None] == jnp.arange(peer_count, dtype=jnp.int32)[None, :]).astype(jnp.int32)
-    rank = jnp.sum((jnp.cumsum(onehot, axis=0) - onehot) * onehot, axis=1)
-    slots = owners * capacity + rank
-    sources = jnp.full((peer_count * capacity,), element_count, jnp.int32)
-    sources = sources.at[slots].set(jnp.arange(element_count, dtype=jnp.int32))
+    same = owners[:, None] == owners[None, :]
+    earlier = lax.broadcasted_iota(jnp.int32, same.shape, 0) > lax.broadcasted_iota(
+        jnp.int32, same.shape, 1
+    )
+    rank = jnp.sum((same & earlier).astype(jnp.int32), axis=1)
+    ntend = coupling.shape[0]
+    capacity = forcing.shape[-1] // peer_count
+    outgoing_forcing = forcing[0, 0].reshape(ntend * 4, peer_count, capacity).transpose(1, 2, 0)
+    received = lax.all_to_all(
+        outgoing_forcing, ("gx", "gy"), split_axis=0, concat_axis=0, tiled=True
+    )
+    received = received.reshape(peer_count * capacity, ntend * 4)
+    local_forcing = jnp.take(received, owners * capacity + rank, axis=0)
+    local_forcing = local_forcing.reshape(element_count, ntend, 4)
     nodes = advanced.reshape(fields, elems_x, 4, elems_y, 4, levels).transpose(1, 3, 0, 2, 4, 5)
     nodes = nodes.reshape(element_count, fields, 16, levels)
     weights_in = to_cells.reshape(element_count, 4, 16)
-    sent_nodes, sent_weights = (
-        lax.all_to_all(
-            pack_rows(nodes, sources), ("gx", "gy"), split_axis=0, concat_axis=0, tiled=True
-        ),
-        lax.all_to_all(
-            pack_rows(weights_in, sources), ("gx", "gy"), split_axis=0, concat_axis=0, tiled=True
-        ),
+    cells = jnp.einsum("epn,efnl->efpl", weights_in, nodes, preferred_element_type=jnp.float32)
+    half_levels = levels // 2
+
+    def own_levels(array):
+        return lax.dynamic_slice_in_dim(array, member * half_levels, half_levels, array.ndim - 1)
+
+    mixed = jnp.einsum("sfpl,lm->sfpm", cells, own_levels(vertical_map), precision=highest)
+    response = jnp.einsum("gf,sfpl->sgpl", coupling, jnp.tanh(mixed), precision=highest)
+    damping = own_levels(relaxation)[None, :, None, :] * (
+        own_levels(cells)[:, :ntend] - mixed[:, :ntend]
     )
-    cells = jnp.einsum(
-        "spn,sfnl->sfpl", sent_weights, sent_nodes, preferred_element_type=jnp.float32
-    )
-    local_forcing = forcing[0, 0].transpose(2, 0, 1)
-    column_tend = column_physics(cells, local_forcing, vertical_map, coupling, relaxation)
-    returned = lax.all_to_all(column_tend, ("gx", "gy"), split_axis=0, concat_axis=0, tiled=True)
-    element_tend = jnp.take(returned, slots, axis=0)
-    ntend = element_tend.shape[1]
+    element_tend = (response - damping + local_forcing[..., None]).astype(jnp.bfloat16)
     weights_out = to_nodes.reshape(element_count, 16, 4)
     nodal = jnp.einsum(
         "enp,egpl->egnl", weights_out, element_tend, preferred_element_type=jnp.float32
     )
-    nodal = nodal.reshape(elems_x, elems_y, ntend, 4, 4, levels).transpose(2, 0, 3, 1, 4, 5)
-    nodal = nodal.reshape(ntend, extent_x, extent_y, levels)
+    nodal = nodal.reshape(elems_x, elems_y, ntend, 4, 4, half_levels).transpose(2, 0, 3, 1, 4, 5)
+    nodal = nodal.reshape(ntend, extent_x, extent_y, half_levels)
+    advanced = own_levels(advanced)
     updated = advanced[:ntend].astype(jnp.float32) + dt_physics * nodal
-    result = jnp.concatenate([updated.astype(jnp.bfloat16), advanced[ntend:]], axis=0)
-    half_levels = levels // 2
-    return lax.dynamic_slice_in_dim(result, member * half_levels, half_levels, 3)
+    return jnp.concatenate([updated.astype(jnp.bfloat16), advanced[ntend:]], axis=0)
 
 
 def solution(mesh):

time: 453 us -> 94.9 us (0.21)
  the two profiles are of different devices: /device:TPU:32 before, /device:TPU:1 now
where the time goes in v1:
time: 94.9 us; the launch traced here: 94.7 us
  waiting for transfers between devices  24.9 us (26%)
  other arithmetic  22.5 us (24%)
  starting transfers between devices  21 us (22%)
  matrix products  14.7 us (15%)
  local copies, waits for them, and re-layouts  11.3 us (12%)
    all_to_all x1, waiting for transfers between devices, shards(): lax.all_to_all(outgoing_forcing, ('gx', 'gy'), split_axis=0, concat_axis=...  11.5 us
    ppermute x2, starting transfers between devices, with_halo(): lax.ppermute(head, axis, [((i + 1) % count, i) for i in range(count)])  11.5 us
    select_n x1, other arithmetic, shards(): outgoing = jnp.where(member == 0, rounded, current)  9.86 us
    ppermute x2, waiting for transfers between devices, with_halo(): lax.ppermute(tail, axis, [(i, (i + 1) % count) for i in range(count)])  8.32 us
    all_to_all x1, starting transfers between devices, shards(): lax.all_to_all(outgoing_forcing, ('gx', 'gy'), split_axis=0, concat_axis=...  6.16 us
    ppermute x2, waiting for transfers between devices, with_halo(): lax.ppermute(head, axis, [((i + 1) % count, i) for i in range(count)])  5.1 us
    dot_general x1, matrix products, derivatives(): jnp.einsum('ij,...xejl->...xeil', derivative, blocks, precision=highest)  4.42 us
    dot_general x1, matrix products, derivatives(): jnp.einsum('ij,...ejyl->...eiyl', derivative, blocks, precision=highest)  4.4 us
  transfers between devices with their start and end apart: 6, of which 5 were waited for; matrix products, arithmetic and copies ran while one was open for 5% of the time, Pallas kernels for 0%

profile of v1, /device:TPU:1, one launch (start us, length us, event | category | flops | bytes accessed | tf_op | source)
XLA Modules:
  0.0 94.7 jit_solution(9751862407012101675)
XLA Ops:
  0.0 2.6 %bitcast_convert_fusion = f32[10,32,32,128]{3,2,1,0:T(8,128)S(1)} fusion(bf16[1,10,32,32,128]{4,3,2,1,0:T(8,128)(2,1)} %param.9), kind=kLoop, calls=%fused_computation.28 | loop fusion | flops 1310720 | bytes 7864320 | tf_op jit(solution)/shard_map/convert_element_type | solution.py:79
  2.7 4.4 %fusion.15 = f32[10,8,4,32,128]{4,2,3,1,0:T(4,128)S(1)} fusion(f32[4,4,1,1,1]{1,0,4,3,2:T(4,128)S(1)} %copy-done.6, bf16[10,8,4,32,128]{4,3,2,1,0:T(8,128)(2,1)S(1)} %bitcast.84), kind=kOutput, calls=%fused_computation.31 | convolution fusion | flops 62914560 | bytes 7864384 | tf_op jit(solution)/shard_map/ij,...ejyl->...eiyl/dot_general | solution.py:56
  7.8 4.4 %fusion.39 = f32[4,10,32,8,128]{4,0,3,2,1:T(4,128)S(1)} fusion(f32[4,4,1,1,1]{1,0,4,3,2:T(4,128)S(1)} %copy-done.6, bf16[10,32,8,4,128]{4,3,2,1,0:T(4,128)(2,1)S(1)} %bitcast.85), kind=kOutput, calls=%fused_computation.69 | convolution fusion | flops 62914560 | bytes 7864384 | tf_op jit(solution)/shard_map/ij,...xejl->...xeil/dot_general | solution.py:60
  12.3 1.5 %add_negate_fusion = f32[10,32,32,128]{3,2,1,0:T(8,128)S(1)} fusion(f32[10,32,32,128]{3,2,1,0:T(8,128)S(1)} %bitcast.88, f32[10,32,32,128]{3,2,1,0:T(8,128)S(1)} %bitcast.87, f32[32,32,128]{2,1,0:T(8,128)S(1)} %get-tuple-element.12, f32[32,32,128]{2,1,0:T(8,128)S(1)} %get-tuple-element.11), kind=kLoop, calls=%fused_computation.23 | loop fusion | flops 5242880 | bytes 16777216 | tf_op jit(solution)/shard_map/neg | solution.py:81
  13.7 8.7 %collective-permute-start = (f32[10,1,32,128]{3,2,1,0:T(8,128)S(1)}, f32[10,1,32,128]{3,2,1,0:T(8,128)S(1)}, u32[]{:S(2)}, u32[]{:S(2)}) collective-permute-start(f32[10,1,32,128]{3,2,1,0:T(8,128)S(1)} %get-tuple-element.9), channel_id=1, source_target_pairs={{4,0},{8,4},{12,8},{16,12},{20,16},{24,20},{28,24},{32,28},{36,32}... | collective-permute-start | bytes 491528 | tf_op jit(solution)/shard_map/ppermute | solution.py:21
  22.4 2.9 %collective-permute-done = f32[10,1,32,128]{3,2,1,0:T(8,128)S(1)} collective-permute-done((f32[10,1,32,128]{3,2,1,0:T(8,128)S(1)}, f32[10,1,32,128]{3,2,1,0:T(8,128)S(1)}, u32[]{:S(2)}, u32[]{:S(2)}) %collective-permute-start) | collective-permute-done | bytes 163872 | tf_op jit(solution)/shard_map/ppermute | solution.py:21
  25.3 5.2 %collective-permute-done.1 = f32[10,1,32,128]{3,2,1,0:T(8,128)S(1)} collective-permute-done((f32[10,1,32,128]{3,2,1,0:T(8,128)S(1)}, f32[10,1,32,128]{3,2,1,0:T(8,128)S(1)}, u32[]{:S(2)}, u32[]{:S(2)}) %collective-permute-start.1) | collective-permute-done | bytes 163872 | tf_op jit(solution)/shard_map/ppermute | solution.py:19
  30.5 2.5 %fusion.10 = f32[10,32,32,128]{3,2,1,0:T(8,128)S(1)} fusion(f32[10,32,32,128]{3,2,1,0:T(8,128)S(1)} %add_negate_fusion, f32[10,1,32,128]{3,2,1,0:T(8,128)S(1)} %collective-permute-done.1, f32[10,1,32,128]{3,2,1,0:T(8,128)S(1)} %collective-permute-done, s32[32]{0:T(128)S(1)} %get-tuple-element.15, s32[32]{0:T(128)S(1)} %get-tuple-element.16, ...), kind=kLoop, calls=%fused_computation.18 | loop fusion | flops 14417920 | bytes 10813728 | tf_op jit(solution)/shard_map/jit(_where)/select_n | solution.py:70
  33.0 2.3 %copy-done.2 = f32[10,32,32,128]{3,2,1,0:T(8,128)} copy-done((f32[10,32,32,128]{3,2,1,0:T(8,128)}, f32[10,32,32,128]{3,2,1,0:T(8,128)S(1)}, u32[]{:S(2)}) %copy-start.2) | copy-done | bytes 5242904
  35.7 2.8 %collective-permute-start.2 = (f32[10,32,1,128]{3,2,1,0:T(1,128)S(1)}, f32[10,32,1,128]{3,2,1,0:T(1,128)S(1)}, u32[]{:S(2)}, u32[]{:S(2)}) collective-permute-start(f32[10,32,1,128]{3,2,1,0:T(1,128)S(1)} %get-tuple-element.7), channel_id=1, source_target_pairs={{1,0},{2,1},{3,2},{0,3},{5,4},{6,5},{7,6},{4,7},{9,8},{10,9},{11,1... | collective-permute-start | bytes 491528 | tf_op jit(solution)/shard_map/ppermute | solution.py:21
  38.5 2.2 %collective-permute-done.2 = f32[10,32,1,128]{3,2,1,0:T(1,128)S(1)} collective-permute-done((f32[10,32,1,128]{3,2,1,0:T(1,128)S(1)}, f32[10,32,1,128]{3,2,1,0:T(1,128)S(1)}, u32[]{:S(2)}, u32[]{:S(2)}) %collective-permute-start.2) | collective-permute-done | bytes 163872 | tf_op jit(solution)/shard_map/ppermute | solution.py:21
  40.7 3.1 %collective-permute-done.3 = f32[10,32,1,128]{3,2,1,0:T(1,128)S(1)} collective-permute-done((f32[10,32,1,128]{3,2,1,0:T(1,128)S(1)}, f32[10,32,1,128]{3,2,1,0:T(1,128)S(1)}, u32[]{:S(2)}, u32[]{:S(2)}) %collective-permute-start.3) | collective-permute-done | bytes 163872 | tf_op jit(solution)/shard_map/ppermute | solution.py:19
  43.9 9.9 %bitcast_select_fusion.1 = (bf16[10,32,32,128]{3,2,1,0:T(8,128)(2,1)}, bf16[10,32,32,128]{3,2,1,0:T(8,128)(2,1)}) fusion(bf16[1,10,32,32,128]{4,3,2,1,0:T(8,128)(2,1)S(1)} %copy-done.1, pred[]{:T(512)S(6)} %eq.33, f32[10,32,32,128]{3,2,1,0:T(8,128)} %copy-done.2, f32[10,32,1,128]{3,2,1,0:T(1,128)S(1)} %collective-permute-done.3, ...), kind=kLoop, calls=%fused_computation.27 | loop fusion | flops 17039360 | bytes 13435169 | tf_op jit(solution)/shard_map/jit(_where)/select_n | solution.py:87
  53.7 3.3 %collective-permute-start.4 = (bf16[10,32,32,128]{3,2,1,0:T(8,128)(2,1)}, bf16[10,32,32,128]{3,2,1,0:T(8,128)(2,1)}, u32[]{:S(2)}, u32[]{:S(2)}) collective-permute-start(bf16[10,32,32,128]{3,2,1,0:T(8,128)(2,1)} %get-tuple-element.5), channel_id=1, source_target_pairs={{0,128},{128,0},{1,129},{129,1},{2,130},{130,2},{3,131},{131,3},{4... | collective-permute-start | bytes 7864328 | tf_op jit(solution)/shard_map/ppermute | solution.py:29
  57.0 1.3 %copy.35 = f32[1,1,8,4,256]{3,2,4,1,0:T(8,128)} copy(f32[1,1,8,4,256]{4,3,2,1,0:T(4,128)S(1)} %copy-done.5) | data formatting | bytes 65536 | tf_op args[4]
  58.4 2.3 %reshape_squeeze.3 = f32[32,128,2]{0,2,1:T(2,128)} reshape(f32[1,1,8,4,256]{3,2,4,1,0:T(8,128)} %copy.35) | data formatting | bytes 65536 | tf_op jit(solution)/shard_map/reshape;squeeze | solution.py:106
  60.7 6.2 %all-to-all-start = ((f32[128,2,32]{2,1,0:T(2,128)}), f32[128,2,32]{2,1,0:T(2,128)S(1)}, u32[]{:S(2)}, u32[]{:S(2)}) async-start(f32[128,2,32]{2,1,0:T(2,128)} %bitcast.26), calls=%async_computation | async-start | bytes 262144 | tf_op jit(solution)/shard_map/all_to_all | solution.py:107
  67.2 11.5 %all-to-all-done = f32[128,2,32]{2,1,0:T(2,128)S(1)} async-done(((f32[128,2,32]{2,1,0:T(2,128)}), f32[128,2,32]{2,1,0:T(2,128)S(1)}, u32[]{:S(2)}, u32[]{:S(2)}) %all-to-all-start) | async-done | bytes 32800 | tf_op jit(solution)/shard_map/all_to_all | solution.py:107
  79.6 3.1 %add_convert_fusion = bf16[10,32,32,128]{3,2,1,0:T(8,128)(2,1)S(1)} fusion(bf16[10,32,32,128]{3,2,1,0:T(8,128)(2,1)} %collective-permute-done.4, bf16[1,10,32,32,128]{4,3,2,1,0:T(8,128)(2,1)S(1)} %copy-done.1, bf16[10,32,32,128]{3,2,1,0:T(8,128)(2,1)} %get-tuple-element.6, pred[]{:T(512)S(6)} %eq.33), kind=kLoop, calls=%fused_computation.22 | loop fusion | flops 9175040 | bytes 10485761 | tf_op jit(solution)/shard_map/convert_element_type | solution.py:93
  84.9 1.3 %fusion.38 = (f32[64,10,4,64]{3,0,2,1:T(8,128)S(1)}, f32[64,10,4,64]{3,0,2,1:T(8,128)S(1)}) fusion(f32[128,128]{1,0:T(8,128)S(1)} %copy-done.4, s32[]{:T(128)S(6)} %select_n.84, f32[64,10,4,128]{3,2,1,0:T(4,128)S(1)} %bitcast.91), kind=kOutput, calls=%fused_computation.68 | convolution fusion | flops 251658240 | bytes 2686980 | tf_op jit(solution)/shard_map/sfpl,lm->sfpm/dot_general | solution.py:122
  86.3 2.5 %fusion.18 = f32[64,4,64,8]{2,3,1,0:T(8,128)S(1)} fusion(f32[64,10,4,64]{3,0,2,1:T(8,128)S(1)} %get-tuple-element.13, f32[8,10]{1,0:T(8,128)S(1)} %copy-done.7), kind=kOutput, calls=%fused_computation.33 | convolution fusion | flops 15728640 | bytes 1179968 | tf_op jit(solution)/shard_map/gf,sfpl->sgpl/dot_general | solution.py:123
  88.8 1.7 %convolution_multiply_fusion = f32[64,8,64,16]{2,3,1,0:T(8,128)S(1)} fusion(bf16[64,16,4,1]{1,2,3,0:T(4,128)(2,1)S(1)} %bitcast.83, f32[64,10,4,64]{3,2,1,0:T(4,128)S(1)} %dynamic-slice_bitcast_fusion, f32[64,8,4,64]{3,0,2,1:T(8,128)S(1)} %slice.69, f32[64,4,64,8]{2,3,1,0:T(8,128)S(1)} %fusion.18, f32[64,8,4]{2,1,0:T(8,128)S(1)} %copy.37, ...), kind=kOutput, calls=%fused_computation.32 | convolution fusion | flops 5373952 | bytes 5574656 | tf_op jit(solution)/shard_map/enp,egpl->egnl/dot_general | solution.py:129
  90.5 1.2 %copy.38 = f32[8,8,4,8,4,64]{5,4,3,2,1,0:T(4,128)S(1)} copy(f32[8,8,4,8,4,64]{5,4,2,0,3,1:T(4,128)S(1)} %bitcast.89) | data formatting | bytes 4194304 | tf_op jit(solution)/shard_map/mul | solution.py:135
  92.7 2.0 %pad_maximum_fusion.4 = bf16[10,32,32,64]{3,2,1,0:T(8,128)(2,1)} fusion(bf16[2,32,32,64]{3,2,1,0:T(8,128)(2,1)S(1)} %constant_dynamic-slice_fusion.1, bf16[8,32,32,64]{3,2,1,0:T(8,128)(2,1)S(1)} %add_convert_fusion.1), kind=kLoop, calls=%fused_computation.25 | loop fusion | flops 655360 | bytes 2621440 | tf_op jit(solution)/shard_map/concatenate | solution.py:136
  (43 shorter events, 5.5 us)
Async XLA Ops:
  0.0 88.8 %copy-start = (bf16[8,8,16,4]{2,3,1,0:T(4,128)(2,1)S(1)}, bf16[8,8,16,4]{2,3,1,0:T(4,128)(2,1)}, u32[]{:S(2)}) copy-start(bf16[8,8,16,4]{2,3,1,0:T(4,128)(2,1)} %param.11) | copy-start | bytes 24580
  0.0 2.7 %copy-start.6 = (f32[4,4,1,1,1]{1,0,4,3,2:T(4,128)S(1)}, f32[4,4,1,1,1]{1,0,4,3,2:T(4,128)}, u32[]{:S(2)}) copy-start(f32[4,4,1,1,1]{1,0,4,3,2:T(4,128)} %constant.63) | copy-start | bytes 196
  0.0 2.7 %copy-start.1 = (bf16[1,10,32,32,128]{4,3,2,1,0:T(8,128)(2,1)S(1)}, bf16[1,10,32,32,128]{4,3,2,1,0:T(8,128)(2,1)}, u32[]{:S(2)}) copy-start(bf16[1,10,32,32,128]{4,3,2,1,0:T(8,128)(2,1)} %param.9) | copy-start | bytes 7864324
  13.7 11.5 %collective-permute-start = (f32[10,1,32,128]{3,2,1,0:T(8,128)S(1)}, f32[10,1,32,128]{3,2,1,0:T(8,128)S(1)}, u32[]{:S(2)}, u32[]{:S(2)}) collective-permute-start(f32[10,1,32,128]{3,2,1,0:T(8,128)S(1)} %get-tuple-element.9), channel_id=1, source_target_pairs={{4,0},{8,4},{12,8},{16,12},{20,16},{24,20},{28,24},{32,28},{36,32}... | collective-permute-start | bytes 491528 | tf_op jit(solution)/shard_map/ppermute | solution.py:21
  22.4 8.1 %collective-permute-start.1 = (f32[10,1,32,128]{3,2,1,0:T(8,128)S(1)}, f32[10,1,32,128]{3,2,1,0:T(8,128)S(1)}, u32[]{:S(2)}, u32[]{:S(2)}) collective-permute-start(f32[10,1,32,128]{3,2,1,0:T(8,128)S(1)} %get-tuple-element.10), channel_id=1, source_target_pairs={{0,4},{4,8},{8,12},{12,16},{16,20},{20,24},{24,28},{28,32},{32,36}... | collective-permute-start | bytes 491528 | tf_op jit(solution)/shard_map/ppermute | solution.py:19
  33.0 2.3 %copy-start.2 = (f32[10,32,32,128]{3,2,1,0:T(8,128)}, f32[10,32,32,128]{3,2,1,0:T(8,128)S(1)}, u32[]{:S(2)}) copy-start(f32[10,32,32,128]{3,2,1,0:T(8,128)S(1)} %fusion.10) | copy-start | bytes 15728644
  35.7 5.1 %collective-permute-start.2 = (f32[10,32,1,128]{3,2,1,0:T(1,128)S(1)}, f32[10,32,1,128]{3,2,1,0:T(1,128)S(1)}, u32[]{:S(2)}, u32[]{:S(2)}) collective-permute-start(f32[10,32,1,128]{3,2,1,0:T(1,128)S(1)} %get-tuple-element.7), channel_id=1, source_target_pairs={{1,0},{2,1},{3,2},{0,3},{5,4},{6,5},{7,6},{4,7},{9,8},{10,9},{11,1... | collective-permute-start | bytes 491528 | tf_op jit(solution)/shard_map/ppermute | solution.py:21
  38.5 5.4 %collective-permute-start.3 = (f32[10,32,1,128]{3,2,1,0:T(1,128)S(1)}, f32[10,32,1,128]{3,2,1,0:T(1,128)S(1)}, u32[]{:S(2)}, u32[]{:S(2)}) collective-permute-start(f32[10,32,1,128]{3,2,1,0:T(1,128)S(1)} %get-tuple-element.8), channel_id=1, source_target_pairs={{0,1},{1,2},{2,3},{3,0},{4,5},{5,6},{6,7},{7,4},{8,9},{9,10},{10,1... | collective-permute-start | bytes 491528 | tf_op jit(solution)/shard_map/ppermute | solution.py:19
  38.5 18.5 %copy-start.5 = (f32[1,1,8,4,256]{4,3,2,1,0:T(4,128)S(1)}, f32[1,1,8,4,256]{4,3,2,1,0:T(4,128)}, u32[]{:S(2)}) copy-start(f32[1,1,8,4,256]{4,3,2,1,0:T(4,128)} %param.13) | copy-start | bytes 98308
  38.5 28.4 %copy-start.9 = (s32[1,1,64,1]{2,3,1,0:T(1,128)S(1)}, s32[1,1,64,1]{2,3,1,0:T(1,128)}, u32[]{:S(2)}) copy-start(s32[1,1,64,1]{2,3,1,0:T(1,128)} %param.12) | copy-start | bytes 772
  38.5 28.6 %copy-start.8 = (f32[8,128]{1,0:T(8,128)S(1)}, f32[8,128]{1,0:T(8,128)}, u32[]{:S(2)}) copy-start(f32[8,128]{1,0:T(8,128)} %param.16) | copy-start | bytes 12292
  53.7 25.8 %collective-permute-start.4 = (bf16[10,32,32,128]{3,2,1,0:T(8,128)(2,1)}, bf16[10,32,32,128]{3,2,1,0:T(8,128)(2,1)}, u32[]{:S(2)}, u32[]{:S(2)}) collective-permute-start(bf16[10,32,32,128]{3,2,1,0:T(8,128)(2,1)} %get-tuple-element.5), channel_id=1, source_target_pairs={{0,128},{128,0},{1,129},{129,1},{2,130},{130,2},{3,131},{131,3},{4... | collective-permute-start | bytes 7864328 | tf_op jit(solution)/shard_map/ppermute | solution.py:29
  60.7 18.0 %all-to-all-start = ((f32[128,2,32]{2,1,0:T(2,128)}), f32[128,2,32]{2,1,0:T(2,128)S(1)}, u32[]{:S(2)}, u32[]{:S(2)}) async-start(f32[128,2,32]{2,1,0:T(2,128)} %bitcast.26), calls=%async_computation | async-start | bytes 262144 | tf_op jit(solution)/shard_map/all_to_all | solution.py:107
  82.7 1.0 %copy-start.3 = (bf16[8,8,4,16]{3,2,1,0:T(4,128)(2,1)S(1)}, bf16[8,8,4,16]{3,2,1,0:T(4,128)(2,1)}, u32[]{:S(2)}) copy-start(bf16[8,8,4,16]{3,2,1,0:T(4,128)(2,1)} %param.10) | copy-start | bytes 24580
  83.7 1.3 %copy-start.4 = (f32[128,128]{1,0:T(8,128)S(1)}, f32[128,128]{1,0:T(8,128)}, u32[]{:S(2)}) copy-start(f32[128,128]{1,0:T(8,128)} %param.14) | copy-start | bytes 196612
  84.2 2.1 %copy-start.7 = (f32[8,10]{1,0:T(8,128)S(1)}, f32[8,10]{1,0:T(8,128)}, u32[]{:S(2)}) copy-start(f32[8,10]{1,0:T(8,128)} %param.15) | copy-start | bytes 964

commit v2 on v1

v2 whole, which is shorter than its diff:
```python
import functools

import jax
import jax.numpy as jnp
import numpy as np
from jax import lax
from jax.experimental import pallas as pl
from jax.experimental.pallas import tpu as pltpu
from jax.sharding import PartitionSpec as P

f32 = jnp.float32
bf16 = jnp.bfloat16
MESH = pl.DeviceIdType.MESH
HBM = pl.BlockSpec(memory_space=pl.ANY)
VMEM = pl.BlockSpec(memory_space=pltpu.VMEM)
SMEM = pl.BlockSpec(memory_space=pltpu.SMEM)

NF, NTEND, LEV = 10, 8, 128
PAIRS = NF // 2
XROWS, YROWS = 16, 32
BLOCKS = XROWS // 4
NODES = 4 * YROWS
CELLS = YROWS
CX, CZ, CY = 4, 8, 4
DT_DYN, DT_PHY = 0.1, 0.25


def gll_matrix():
    points = np.array([-1.0, -1.0 / np.sqrt(5.0), 1.0 / np.sqrt(5.0), 1.0])
    bary = np.ones(4)
    for i in range(4):
        for j in range(4):
            if i != j:
                bary[i] /= points[i] - points[j]
    matrix = np.zeros((4, 4))
    for i in range(4):
        for j in range(4):
            if i != j:
                matrix[i, j] = bary[j] / bary[i] / (points[i] - points[j])
        matrix[i, i] = -np.sum(matrix[i])
    return matrix


def constants():
    d = gll_matrix()
    weight1 = np.array([0.5, 1.0, 1.0, 0.5])
    weight = np.kron(weight1, np.tile(weight1, YROWS // 4))
    along_x = np.kron(d, np.eye(YROWS))
    along_y = np.kron(np.eye(4 * YROWS // 4), d)
    both = np.concatenate([along_x, along_y]) * (-DT_DYN * np.tile(weight, 2))[:, None]
    high = np.asarray(both, np.float32).astype(jnp.bfloat16)
    low = (both - high.astype(np.float64)).astype(np.float32).astype(jnp.bfloat16)
    derive = np.concatenate([high, low], axis=1)
    share = np.eye(YROWS)
    for y in range(3, YROWS - 1, 4):
        share[y, y + 1] = share[y + 1, y] = 1.0
    advance = np.concatenate([np.kron(np.eye(4), share), np.eye(NODES)], axis=1)
    edges = np.zeros((BLOCKS, NODES, 2 * XROWS))
    for block in range(BLOCKS):
        for i in range(4):
            edges[block, i * YROWS, 4 * block + i] = 1.0
            edges[block, i * YROWS + YROWS - 1, XROWS + 4 * block + i] = 1.0
    return derive, advance.astype(jnp.bfloat16), edges.astype(jnp.bfloat16)


def iota(shape, dim):
    return lax.broadcasted_iota(jnp.int32, shape, dim)


def halves(x):
    high = x.astype(bf16)
    return high, (x - high.astype(f32)).astype(bf16)


def mm(a, b):
    return jnp.dot(a, b, preferred_element_type=f32)


def mm_nt(a, b):
    return lax.dot_general(a, b, (((1,), (1,)), ((), ())), preferred_element_type=f32)


def mm2(a, b):
    high, low = halves(b)
    return mm(a, high) + mm(a, low)


def main_kernel(
    sec, tc, tn, own, frc, vmap, cpl, rel, derive_h, advance_h, edges_h,
    packed, landed,
    both, adv, advd, wind, xlo, xhi, yrow, ysend, ylo, yhi, halo, csend, crecv,
    tc_v, tn_v, own_v, frc_v, v_v, rel_v, derive, advance, edges,
    f2, ts, win, wout, vv, fa, fb1, fs2, fb2, fs3, fb3, fbc, cells, split, mixed, act, tend,
    small_sem, local_sem, in_send, in_recv, e_send, e_recv, c_send, c_recv, f_send, f_recv,
    o_send, o_recv,
):
    m, gx, gy = lax.axis_index("grp"), lax.axis_index("gx"), lax.axis_index("gy")
    z, x = gx // CX, gx % CX
    ngx = CX * CZ
    other = 1 - m
    partner = (other, gx, gy)
    left_gx, right_gx = (gx + ngx - other) % ngx, (gx + m) % ngx
    cross_gx = (gx + ngx + 2 * m - 1) % ngx
    down, up = (gy + CY - 1) % CY, (gy + 1) % CY

    barrier = pltpu.get_barrier_semaphore()
    peers = [partner, (other, cross_gx, gy)]
    peers += [(other, a, b) for a in (gx, cross_gx) for b in (down, up)]
    peers += [(m, gx, (gy + j) % CY) for j in range(1, CY)]
    peers += [(m, z * CX + (x + j) % CX, gy) for j in range(1, CX)]
    peers += [(m, ((z + j) % CZ) * CX + x, gy) for j in range(1, CZ)]
    for peer in peers:
        pl.semaphore_signal(barrier, inc=1, device_id=peer, device_id_type=MESH)

    def local_in(p):
        return pltpu.make_async_copy(
            sec.at[0, pl.ds(2 * p, 2), pl.ds(m * XROWS, XROWS)],
            both.at[m, pl.ds(2 * p, 2)],
            local_sem.at[p],
        )

    def remote_in(p):
        return pltpu.make_async_remote_copy(
            sec.at[0, pl.ds(2 * p, 2), pl.ds(other * XROWS, XROWS)],
            both.at[m, pl.ds(2 * p, 2)],
            in_send.at[p], in_recv.at[p], device_id=partner, device_id_type=MESH,
        )

    def remote_in_wait(p):
        pltpu.make_async_remote_copy(
            both.at[other, pl.ds(2 * p, 2)],
            both.at[other, pl.ds(2 * p, 2)],
            in_send.at[p], in_recv.at[p], device_id=partner, device_id_type=MESH,
        ).wait_recv()

    small = [
        pltpu.make_async_copy(src, dst, small_sem.at[k])
        for k, (src, dst) in enumerate([
            (frc, frc_v), (derive_h, derive), (advance_h, advance), (edges_h, edges),
            (tc.at[pl.ds(m * BLOCKS, BLOCKS)], tc_v), (tn.at[pl.ds(m * BLOCKS, BLOCKS)], tn_v),
            (own, own_v), (vmap, v_v), (rel, rel_v),
        ])
    ]
    small[0].start()
    for p in range(PAIRS):
        local_in(p).start()
    for copy in small[1:]:
        copy.start()

    pl.semaphore_wait(barrier, len(peers))
    for p in range(PAIRS):
        remote_in(p).start()

    small[0].wait()
    for g in range(NTEND):
        f2[4 * g:4 * g + 4, :] = frc_v[g]
    source = iota((128, 256), 0)
    source = 2 * ((source % 32) * CY + source // 32)
    slot = iota((128, 256), 1)
    table = f2[...]
    rows_high, rows_low = halves(table)
    empty = jnp.zeros((32, 256), bf16)
    total = jnp.zeros((128, 128), f32)
    for r in range(2):
        pick = (slot == source + r).astype(f32).astype(bf16)
        for part in (rows_high, rows_low):
            stack = [empty] * 4
            stack[r] = part
            total = total + mm_nt(pick, jnp.concatenate(stack, axis=0))
    fa[...] = total

    def hops(k, src, dst, me, count, rows, device_of):
        out, arrive = [], []
        for j in range(1, count):
            to, frm = (me + j) % count, (me + count - j) % count
            for lst, dst_index in ((out, me), (arrive, frm)):
                lst.append(pltpu.make_async_remote_copy(
                    src.at[pl.ds(pl.multiple_of(to * rows, rows), rows)],
                    dst.at[pl.ds(pl.multiple_of(dst_index * rows, rows), rows)],
                    f_send.at[k, j], f_recv.at[k, j],
                    device_id=device_of(to), device_id_type=MESH,
                ))
        for copy in out:
            copy.start()
        mine = pl.ds(pl.multiple_of(me * rows, rows), rows)
        dst[mine, :] = src[mine, :]
        return out, arrive

    hop1, come1 = hops(0, fa, fb1, gy, CY, 32, lambda t: (m, gx, t))

    for copy in small[1:]:
        copy.wait()
    spread = (iota((16, 128), 0) == (iota((16, 128), 1) // 32) * 4 + iota((16, 128), 1) % 4)
    spread = spread.astype(f32).astype(bf16)
    inside = (iota((128, 128), 0) // 4) % 8 == (iota((128, 128), 1) // 4) % 8
    for k, ref in enumerate((tc_v, tn_v)):
        for block in range(BLOCKS):
            for ey in range(8):
                row = block * 32 + ey * 4
                ts[row:row + 4, :] = ref[block, ey].astype(f32)
        wide = jnp.where(inside, mm(ts[...].astype(bf16), spread), 0.0)
        if k == 0:
            win[...] = wide.astype(bf16)
        else:
            turned = jnp.transpose(wide * DT_PHY)
            eye = (iota((128, 128), 0) == iota((128, 128), 1)).astype(f32).astype(bf16)
            for block in range(BLOCKS):
                moved = turned if block == 0 else pltpu.roll(turned, 128 - 32 * block, 1)
                wout[block, :, 0:128] = eye
                wout[block, :, 128:256] = moved.astype(bf16)
    v_high, v_low = halves(v_v[...])
    vv[0:128, 0:128] = v_high
    vv[128:256, 0:128] = v_high
    vv[0:128, 128:256] = v_low
    vv[128:256, 128:256] = jnp.zeros((128, 128), bf16)

    for copy in come1:
        copy.wait_recv()
    for k in range(CX):
        fs2[32 * k:32 * k + 32, :] = fb1[pl.ds(k, 32, stride=CX), :]
    hop2, come2 = hops(1, fs2, fb2, x, CX, 32, lambda t: (m, z * CX + t, gy))

    def edge_copies(p):
        fields = pl.ds(2 * p, 2)
        return [
            pltpu.make_async_remote_copy(
                src, dst, e_send.at[k, p], e_recv.at[k, p], device_id=to, device_id_type=MESH
            )
            for k, (src, dst, to) in enumerate([
                (adv.at[fields, 0], xhi.at[fields], (other, left_gx, gy)),
                (adv.at[fields, XROWS - 1], xlo.at[fields], (other, right_gx, gy)),
                (ysend.at[0, fields], yhi.at[fields], (m, gx, down)),
                (ysend.at[1, fields], ylo.at[fields], (m, gx, up)),
            ])
        ]

    def section_pair(p, carry):
        @pl.when(m == 0)
        def _():
            local_in(p).wait()

        @pl.when(m == 1)
        def _():
            remote_in_wait(p)

        @pl.when(p == 0)
        def _():
            for k in range(2):
                for block in range(BLOCKS):
                    rows = both[0, k, 4 * block:4 * block + 4].reshape(NODES, LEV)
                    wind[k, block] = rows.astype(f32)

        def put(row, value, raw):
            for k in range(2):
                part = value[:, k * LEV:(k + 1) * LEV]
                f = 2 * p + k
                adv[f, row] = part.astype(bf16)
                for side, edge in ((0, 0), (1, YROWS - 1)):
                    line = part[edge:edge + 1, :]
                    yrow[side, k, row:row + 1, :] = line
                    if raw is not None:
                        csend[2 * raw + side, pl.ds(f, 1), :] = line

        last = None
        for block in range(BLOCKS):
            pair = [both[0, 2 * p + k, 4 * block:4 * block + 4].reshape(NODES, LEV) for k in range(2)]
            once = jnp.concatenate(pair, axis=1)
            slopes = mm(derive[...], jnp.concatenate([once, once], axis=0))
            u, v = wind[0, block], wind[1, block]
            value = jnp.concatenate([u, u], axis=1) * slopes[:NODES]
            value = value + jnp.concatenate([v, v], axis=1) * slopes[NODES:]
            first = value[:YROWS]
            if block == 0:
                put(0, first, 0)
            else:
                shared = last + first
                put(4 * block - 1, shared, None)
                put(4 * block, shared, None)
            put(4 * block + 1, value[YROWS:2 * YROWS], None)
            put(4 * block + 2, value[2 * YROWS:3 * YROWS], None)
            last = value[3 * YROWS:]
        put(XROWS - 1, last, 1)
        for side in range(2):
            for k in range(2):
                ysend[side, 2 * p + k] = yrow[side, k].astype(bf16)
        for copy in edge_copies(p):
            copy.start()
        return carry

    lax.fori_loop(0, PAIRS, section_pair, 0)

    corners = []
    for xs in range(2):
        for ys in range(2):
            corners.append(pltpu.make_async_remote_copy(
                csend.at[2 * xs + ys], crecv.at[3 - 2 * xs - ys],
                c_send.at[2 * xs + ys], c_recv.at[2 * xs + ys],
                device_id=(other, (left_gx, right_gx)[xs], (down, up)[ys]), device_id_type=MESH,
            ))
    for copy in corners:
        copy.start()

    for copy in come2:
        copy.wait_recv()
    for k in range(CZ):
        fs3[16 * k:16 * k + 16, :] = fb2[pl.ds(k, 16, stride=CZ), :]
    hop3, come3 = hops(2, fs3, fb3, z, CZ, 16, lambda t: (m, t * CX + x, gy))

    owned = (iota((128, 64), 0) == own_v[...]).astype(f32)
    before = (iota((64, 64), 0) < iota((64, 64), 1)).astype(f32).astype(bf16)
    rank = mm(owned.astype(bf16), before)
    mine = (iota((128, 64), 1) == m * 32 + iota((128, 64), 0) // 4).astype(f32).astype(bf16)
    from0 = mm_nt(mine, jnp.where(rank < 0.5, owned, 0.0).astype(bf16)).astype(bf16)
    from1 = mm_nt(mine, jnp.where(rank < 0.5, 0.0, owned).astype(bf16)).astype(bf16)

    for copy in come3:
        copy.wait_recv()
    table = fb3[...]
    lines = mm2(from0, table) + mm2(from1, pltpu.roll(table, 96, 1))
    lane = iota((128, 128), 1)
    lines = jnp.where((lane < 32) & (lane % 4 == iota((128, 128), 0) % 4), lines, 0.0)
    high = lines.astype(bf16).astype(f32)
    lines = (high + pltpu.roll(lines - high, 32, 1)).astype(bf16)
    group = jnp.where(iota((128, 128), 0) < 64, (iota((128, 128), 0) // 4) % 8, 8)
    for g in range(NTEND):
        fbc[g] = mm(lines, (group == g).astype(f32).astype(bf16))

    for copy in corners:
        copy.wait_recv()

    def halo_pair(p, carry):
        for copy in edge_copies(p):
            copy.wait_recv()

        @pl.when(m == 1)
        def _():
            local_in(p).wait()

        @pl.when(m == 0)
        def _():
            remote_in_wait(p)

        at = iota((XROWS, LEV), 0)
        for k in range(2):
            f = 2 * p + k
            for side, ref in ((0, ylo), (1, yhi)):
                first = jnp.broadcast_to(crecv[side, pl.ds(f, 1), :], (XROWS, LEV))
                final = jnp.broadcast_to(crecv[2 + side, pl.ds(f, 1), :], (XROWS, LEV))
                value = ref[f].astype(f32)
                value = value + jnp.where(at == 0, first, jnp.where(at == XROWS - 1, final, 0.0))
                halo[f, side * XROWS:(side + 1) * XROWS, :] = value.astype(bf16)
        return carry

    lax.fori_loop(0, PAIRS, halo_pair, 0)

    lower = iota((YROWS, LEV), 1) < LEV // 2

    def pack(block, f, value):
        for i in range(2):
            a = value[i * YROWS:(i + 1) * YROWS]
            b = value[(i + 2) * YROWS:(i + 3) * YROWS]
            packed[0, block, f, i] = jnp.where(lower, a, pltpu.roll(b, 64, 1)).astype(bf16)
            packed[1, block, f, i] = jnp.where(lower, pltpu.roll(a, 64, 1), b).astype(bf16)

    def out_copy(block):
        return pltpu.make_async_remote_copy(
            packed.at[other, block], landed.at[block], o_send.at[block], o_recv.at[block],
            device_id=partner, device_id_type=MESH,
        )

    for block in (1, 2, 0, 3):
        weights = win[32 * block:32 * block + 32, :]

        def advance_pair(p, carry):
            parts, starts = [], []
            for k in range(2):
                f = 2 * p + k
                rows = [adv[f, 4 * block + i] for i in range(4)]
                if block == 0:
                    rows[0] = (rows[0].astype(f32) + xlo[f].astype(f32)).astype(bf16)
                if block == BLOCKS - 1:
                    rows[3] = (rows[3].astype(f32) + xhi[f].astype(f32)).astype(bf16)
                start = both[1, f, 4 * block:4 * block + 4].reshape(NODES, LEV)
                parts.append(jnp.concatenate(rows + [start], axis=0))
                starts.append(halo[f])
            value = mm(advance[...], jnp.concatenate(parts, axis=1))
            value = value + mm(edges[block], jnp.concatenate(starts, axis=1))
            value = value.astype(bf16)
            got = mm(weights, value)
            for k in range(2):
                f = 2 * p + k
                advd[f, block] = value[:, k * LEV:(k + 1) * LEV]
                one = got[:, k * LEV:(k + 1) * LEV]
                cells[f] = one
                high, low = halves(one)
                split[f, :, 0:LEV] = high
                split[f, :, LEV:2 * LEV] = low
            return carry

        lax.fori_loop(0, PAIRS, advance_pair, 0)

        def mix_pair(p, carry):
            lhs = split[pl.ds(2 * p, 2)].reshape(2 * CELLS, 2 * LEV)
            got = mm(lhs, vv[...])
            got = got[:, :LEV] + got[:, LEV:]
            warm = jnp.tanh(got)
            for k in range(2):
                mixed[2 * p + k] = got[k * CELLS:(k + 1) * CELLS]
                act[2 * p + k] = warm[k * CELLS:(k + 1) * CELLS]
            return carry

        lax.fori_loop(0, PAIRS, mix_pair, 0, unroll=True)

        for g in range(NTEND):
            acc = fbc[g, 32 * block:32 * block + 32, :]
            for f in range(NF):
                acc = acc + cpl[g, f] * act[f]
            acc = acc - rel_v[g:g + 1, :] * (cells[g] - mixed[g])
            tend[g] = acc.astype(bf16)

        def update_pair(p, carry):
            parts = [
                jnp.concatenate([advd[2 * p + k, block], tend[2 * p + k]], axis=0) for k in range(2)
            ]
            value = mm(wout[block, :, 0:NODES + CELLS], jnp.concatenate(parts, axis=1))
            for k in range(2):
                pack(block, 2 * p + k, value[:, k * LEV:(k + 1) * LEV])
            return carry

        lax.fori_loop(0, NTEND // 2, update_pair, 0)
        for f in range(NTEND, NF):
            pack(block, f, advd[f, block].astype(f32))
        out_copy(block).start()

    for p in range(PAIRS):
        remote_in(p).wait_send()
        for copy in edge_copies(p):
            copy.wait_send()
    for copy in corners + hop1 + hop2 + hop3:
        copy.wait_send()
    for block in range(BLOCKS):
        out_copy(block).wait_send()
        out_copy(block).wait_recv()


def main_call(args):
    v = pltpu.VMEM
    packed_shape = (BLOCKS, NF, 2, YROWS, LEV)
    dma = pltpu.SemaphoreType.DMA
    scratch = [
        v((2, NF, XROWS, YROWS, LEV), bf16),
        v((NF, XROWS, YROWS, LEV), bf16),
        v((NF, BLOCKS, NODES, LEV), bf16),
        v((2, BLOCKS, NODES, LEV), f32),
        v((NF, YROWS, LEV), bf16),
        v((NF, YROWS, LEV), bf16),
        v((2, 2, XROWS, LEV), f32),
        v((2, NF, XROWS, LEV), bf16),
        v((NF, XROWS, LEV), bf16),
        v((NF, XROWS, LEV), bf16),
        v((NF, 2 * XROWS, LEV), bf16),
        v((4, 16, LEV), f32),
        v((4, 16, LEV), f32),
        v((BLOCKS, 8, 4, 16), bf16),
        v((BLOCKS, 8, 4, 16), bf16),
        v((1, 64), jnp.int32),
        v((NTEND, 4, 256), f32),
        v((LEV, LEV), f32),
        v((NTEND, LEV), f32),
        v((2 * NODES, 2 * NODES), bf16),
        v((NODES, 2 * NODES), bf16),
        v((BLOCKS, NODES, 2 * XROWS), bf16),
        v((32, 256), f32),
        v((128, 16), f32),
        v((128, 128), bf16),
        v((BLOCKS, 128, 256), bf16),
        v((256, 256), bf16),
    ]
    scratch += [v((128, 128), f32)] * 6
    scratch += [
        v((NTEND, 128, LEV), f32),
        v((NF, CELLS, LEV), f32),
        v((NF, CELLS, 2 * LEV), bf16),
        v((NF, CELLS, LEV), f32),
        v((NF, CELLS, LEV), f32),
        v((NTEND, CELLS, LEV), bf16),
        dma((9,)), dma((PAIRS,)), dma((PAIRS,)), dma((PAIRS,)),
        dma((4, PAIRS)), dma((4, PAIRS)), dma((4,)), dma((4,)),
        dma((3, CZ)), dma((3, CZ)), dma((BLOCKS,)), dma((BLOCKS,)),
    ]
    in_specs = [HBM] * 11
    in_specs[6] = SMEM
    return pl.pallas_call(
        main_kernel,
        out_shape=(
            jax.ShapeDtypeStruct((2,) + packed_shape, bf16),
            jax.ShapeDtypeStruct(packed_shape, bf16),
        ),
        in_specs=in_specs,
        out_specs=(VMEM, VMEM),
        scratch_shapes=scratch,
        compiler_params=pltpu.CompilerParams(
            collective_id=0, has_side_effects=True, vmem_limit_bytes=40 * 2**20
        ),
    )(*args)


def unpack_kernel(packed, landed, out, stage, sems):
    m = lax.axis_index("grp")

    def copy(k, block):
        rows = (m if k == 0 else 1 - m) * XROWS + 4 * block
        return pltpu.make_async_copy(
            stage.at[k, block], out.at[:, pl.ds(rows, 4)], sems.at[k, block]
        )

    for k in range(2):
        for block in range(BLOCKS):

            def one(f, carry):
                for i in range(2):
                    line = packed[m, block, f, i] if k == 0 else landed[block, f, i]
                    stage[k, block, f, i] = line[:, :LEV // 2]
                    moved = pltpu.roll(line.astype(f32), 64, 1).astype(bf16)
                    stage[k, block, f, i + 2] = moved[:, :LEV // 2]
                return carry

            lax.fori_loop(0, NF, one, 0, unroll=True)
            copy(k, block).start()
    for k in range(2):
        for block in range(BLOCKS):
            copy(k, block).wait()


def unpack_call(packed, landed):
    return pl.pallas_call(
        unpack_kernel,
        out_shape=jax.ShapeDtypeStruct((NF, 2 * XROWS, YROWS, LEV // 2), bf16),
        in_specs=[VMEM, VMEM],
        out_specs=HBM,
        scratch_shapes=[
            pltpu.VMEM((2, BLOCKS, NF, 4, YROWS, LEV // 2), bf16),
            pltpu.SemaphoreType.DMA((2, BLOCKS)),
        ],
        compiler_params=pltpu.CompilerParams(vmem_limit_bytes=24 * 2**20),
    )(packed, landed)


def shards(
    section_levels, to_cells, to_nodes, owner_map, forcing, vertical_map, coupling, relaxation
):
    derive, advance, edges = (jnp.asarray(c) for c in constants())
    packed, landed = main_call((
        section_levels, to_cells, jnp.swapaxes(to_nodes, 2, 3), owner_map.reshape(1, 64),
        forcing[0, 0], vertical_map, coupling, relaxation, derive, advance, edges,
    ))
    return unpack_call(packed, landed)


def solution(mesh):
    in_specs = (
        P("grp", None, "gx", "gy", None),
        P("gx", "gy", None, None),
        P("gx", "gy", None, None),
        P("gx", "gy", None, None),
        P("gx", "gy", None, None, None),
        P(),
        P(),
        P(),
    )
    out_specs = P(None, "gx", "gy", "grp")
    return jax.shard_map(shards, mesh=mesh, in_specs=in_specs, out_specs=out_specs, check_vma=False)
```

time: 94.9 us -> 49.7 us (0.52)
  Pallas kernels: 0 us -> 39.5 us
  waiting for transfers between devices: 24.9 us -> 0 us
  other arithmetic: 22.5 us -> 0 us
  starting transfers between devices: 21 us -> 0 us
  matrix products: 14.7 us -> 0 us
  local copies, waits for them, and re-layouts: 11.3 us -> 9.69 us
    pallas_call x0 -> x2, Pallas kernels: none -> 39.5 us  [the longest x1 37.8 us: main_call(): pl.pallas_call(main_kernel, out_shape=(jax.ShapeDtypeStruct((2,) + packed...]
    ppermute x5 -> x0, starting transfers between devices: 14.8 us -> none  [the longest x2 11.5 us: with_halo(): lax.ppermute(head, axis, [((i + 1) % count, i) for i in range(count)])]
    dot_general x6 -> x0, matrix products: 14.7 us -> none  [the longest x1 4.42 us: derivatives(): jnp.einsum('ij,...xejl->...xeil', derivative, blocks, precision=highest)]
    ppermute x5 -> x0, waiting for transfers between devices: 13.4 us -> none  [the longest x2 8.32 us: with_halo(): lax.ppermute(tail, axis, [(i, (i + 1) % count) for i in range(count)])]
    select_n x4 -> x0, other arithmetic: 12.4 us -> none  [the longest x1 9.86 us: shards(): outgoing = jnp.where(member == 0, rounded, current)]
    all_to_all x1 -> x0, waiting for transfers between devices: 11.5 us -> none  [shards(): lax.all_to_all(outgoing_forcing, ('gx', 'gy'), split_axis=0, concat_axis=...]
    convert_element_type x3 -> x0, other arithmetic: 6.49 us -> none  [the longest x1 3.1 us: shards(): advanced = (initial.astype(jnp.float32) + dt_dynamics * section_rate.asty...]
    all_to_all x1 -> x0, starting transfers between devices: 6.16 us -> none  [shards(): lax.all_to_all(outgoing_forcing, ('gx', 'gy'), split_axis=0, concat_axis=...]
  transfers between devices with their start and end apart: 6 -> 0, of which waited for: 5 -> 0; matrix products, arithmetic and copies ran while one was open for 5% -> 0% of each run, Pallas kernels for 0% -> 0%
where the time goes in v2:
time: 49.7 us; the launch traced here: 49.2 us
  Pallas kernels  39.5 us (79%)
  local copies, waits for them, and re-layouts  9.69 us (19%)
    pallas_call x1, Pallas kernels, main_call(): pl.pallas_call(main_kernel, out_shape=(jax.ShapeDtypeStruct((2,) + packed...  37.8 us
    unnamed x22, local copies, waits for them, and re-layouts  9.69 us
    pallas_call x1, Pallas kernels, unpack_call(): pl.pallas_call(unpack_kernel, out_shape=jax.ShapeDtypeStruct((NF, 2 * XRO...  1.67 us

profile of v2, /device:TPU:1, one launch (start us, length us, event | category | flops | bytes accessed | tf_op | source)
XLA Modules:
  0.0 49.2 jit_solution(3416647480317608854)
XLA Ops:
  0.0 0.0 copy-start
  0.0 1.7 %copy-done = bf16[1,10,32,32,128]{4,3,2,1,0:T(8,128)(2,1)S(1)} copy-done((bf16[1,10,32,32,128]{4,3,2,1,0:T(8,128)(2,1)S(1)}, bf16[1,10,32,32,128]{4,3,2,1,0:T(8,128)(2,1)}, u32[]{:S(2)}) %copy-start) | copy-done | bytes 2621464
  1.7 0.0 copy-start.1
  1.7 0.9 %copy-done.1 = bf16[4,128,32]{2,1,0:T(8,128)(2,1)S(1)} copy-done((bf16[4,128,32]{2,1,0:T(8,128)(2,1)S(1)}, bf16[4,128,32]{2,1,0:T(8,128)(2,1)}, u32[]{:S(2)}) %copy-start.1) | copy-done | bytes 32792
  2.6 0.0 copy-start.2
  2.6 0.9 %copy-done.2 = bf16[256,256]{1,0:T(8,128)(2,1)S(1)} copy-done((bf16[256,256]{1,0:T(8,128)(2,1)S(1)}, bf16[256,256]{1,0:T(8,128)(2,1)}, u32[]{:S(2)}) %copy-start.2) | copy-done | bytes 131096
  3.6 0.0 copy-start.3
  3.6 0.8 %copy-done.3 = bf16[8,8,4,16]{3,2,1,0:T(4,128)(2,1)S(1)} copy-done((bf16[8,8,4,16]{3,2,1,0:T(4,128)(2,1)S(1)}, bf16[8,8,4,16]{3,2,1,0:T(4,128)(2,1)}, u32[]{:S(2)}) %copy-start.3) | copy-done | bytes 8216
  4.4 0.0 copy-start.4
  4.4 0.8 %copy-done.4 = bf16[8,8,16,4]{2,3,1,0:T(4,128)(2,1)S(1)} copy-done((bf16[8,8,16,4]{2,3,1,0:T(4,128)(2,1)S(1)}, bf16[8,8,16,4]{2,3,1,0:T(4,128)(2,1)}, u32[]{:S(2)}) %copy-start.4) | copy-done | bytes 8216
  5.2 0.0 copy-start.5
  5.2 0.8 %copy-done.5 = f32[128,128]{1,0:T(8,128)S(1)} copy-done((f32[128,128]{1,0:T(8,128)S(1)}, f32[128,128]{1,0:T(8,128)}, u32[]{:S(2)}) %copy-start.5) | copy-done | bytes 65560
  6.1 0.0 copy-start.6
  6.1 0.8 %copy-done.6 = bf16[128,256]{1,0:T(8,128)(2,1)S(1)} copy-done((bf16[128,256]{1,0:T(8,128)(2,1)S(1)}, bf16[128,256]{1,0:T(8,128)(2,1)}, u32[]{:S(2)}) %copy-start.6) | copy-done | bytes 65560
  6.9 0.0 copy-start.7
  6.9 0.8 %copy-done.7 = f32[1,1,8,4,256]{4,3,2,1,0:T(4,128)S(1)} copy-done((f32[1,1,8,4,256]{4,3,2,1,0:T(4,128)S(1)}, f32[1,1,8,4,256]{4,3,2,1,0:T(4,128)}, u32[]{:S(2)}) %copy-start.7) | copy-done | bytes 32792
  7.7 0.0 copy-start.8
  7.7 0.7 %copy-done.8 = f32[8,10]{1,0:T(8,128)S(1)} copy-done((f32[8,10]{1,0:T(8,128)S(1)}, f32[8,10]{1,0:T(8,128)}, u32[]{:S(2)}) %copy-start.8) | copy-done | bytes 344
  8.4 0.0 copy-start.9
  8.4 0.7 %copy-done.9 = f32[8,128]{1,0:T(8,128)S(1)} copy-done((f32[8,128]{1,0:T(8,128)S(1)}, f32[8,128]{1,0:T(8,128)}, u32[]{:S(2)}) %copy-start.9) | copy-done | bytes 4120
  9.0 0.0 copy-start.10
  9.0 0.7 %copy-done.10 = s32[1,1,64,1]{2,3,1,0:T(1,128)S(1)} copy-done((s32[1,1,64,1]{2,3,1,0:T(1,128)S(1)}, s32[1,1,64,1]{2,3,1,0:T(1,128)}, u32[]{:S(2)}) %copy-start.10) | copy-done | bytes 280
  9.7 37.8 %shard_map.109 = (bf16[2,4,10,2,32,128]{5,4,3,2,1,0:T(8,128)(2,1)S(1)}, bf16[4,10,2,32,128]{4,3,2,1,0:T(8,128)(2,1)S(1)}) custom-call(bf16[1,10,32,32,128]{4,3,2,1,0:T(8,128)(2,1)S(1)} %copy-done, bf16[8,8,4,16]{3,2,1,0:T(4,128)(2,1)S(1)} %copy-done.3, bf16[8,8,4,16]{3,2,1,0:T(4,128)(2,1)S(1)} %bitcast.3, s32[1,64]{1,0:T(1,128)S(1)} %bitcast.5, ...), custom_call_target="tpu_custom_call" | custom-call | tf_op jit(solution)/shard_map/pallas_call | solution.py:493
  47.5 1.7 %shard_map.110 = bf16[10,32,32,64]{3,2,1,0:T(8,128)(2,1)} custom-call(bf16[2,4,10,2,32,128]{5,4,3,2,1,0:T(8,128)(2,1)S(1)} %get-tuple-element.7.packed, bf16[4,10,2,32,128]{4,3,2,1,0:T(8,128)(2,1)S(1)} %get-tuple-element.8.landed), custom_call_target="tpu_custom_call" | custom-call | tf_op jit(solution)/shard_map/pallas_call | solution.py:536
Async XLA Ops:
  0.0 1.7 %copy-start = (bf16[1,10,32,32,128]{4,3,2,1,0:T(8,128)(2,1)S(1)}, bf16[1,10,32,32,128]{4,3,2,1,0:T(8,128)(2,1)}, u32[]{:S(2)}) copy-start(bf16[1,10,32,32,128]{4,3,2,1,0:T(8,128)(2,1)} %sec.1) | copy-start | bytes 7864324
  1.7 0.9 %copy-start.1 = (bf16[4,128,32]{2,1,0:T(8,128)(2,1)S(1)}, bf16[4,128,32]{2,1,0:T(8,128)(2,1)}, u32[]{:S(2)}) copy-start(bf16[4,128,32]{2,1,0:T(8,128)(2,1)} %constant.8.clone.edges_h) | copy-start | bytes 98308
  2.6 0.9 %copy-start.2 = (bf16[256,256]{1,0:T(8,128)(2,1)S(1)}, bf16[256,256]{1,0:T(8,128)(2,1)}, u32[]{:S(2)}) copy-start(bf16[256,256]{1,0:T(8,128)(2,1)} %constant.6.clone.derive_h) | copy-start | bytes 393220
  3.6 0.8 %copy-start.3 = (bf16[8,8,4,16]{3,2,1,0:T(4,128)(2,1)S(1)}, bf16[8,8,4,16]{3,2,1,0:T(4,128)(2,1)}, u32[]{:S(2)}) copy-start(bf16[8,8,4,16]{3,2,1,0:T(4,128)(2,1)} %tc.1) | copy-start | bytes 24580
  4.4 0.8 %copy-start.4 = (bf16[8,8,16,4]{2,3,1,0:T(4,128)(2,1)S(1)}, bf16[8,8,16,4]{2,3,1,0:T(4,128)(2,1)}, u32[]{:S(2)}) copy-start(bf16[8,8,16,4]{2,3,1,0:T(4,128)(2,1)} %param.13) | copy-start | bytes 24580
  5.2 0.8 %copy-start.5 = (f32[128,128]{1,0:T(8,128)S(1)}, f32[128,128]{1,0:T(8,128)}, u32[]{:S(2)}) copy-start(f32[128,128]{1,0:T(8,128)} %vmap.1) | copy-start | bytes 196612
  6.1 0.8 %copy-start.6 = (bf16[128,256]{1,0:T(8,128)(2,1)S(1)}, bf16[128,256]{1,0:T(8,128)(2,1)}, u32[]{:S(2)}) copy-start(bf16[128,256]{1,0:T(8,128)(2,1)} %constant.7.clone.advance_h) | copy-start | bytes 196612
  6.9 0.8 %copy-start.7 = (f32[1,1,8,4,256]{4,3,2,1,0:T(4,128)S(1)}, f32[1,1,8,4,256]{4,3,2,1,0:T(4,128)}, u32[]{:S(2)}) copy-start(f32[1,1,8,4,256]{4,3,2,1,0:T(4,128)} %param.15) | copy-start | bytes 98308
  7.7 0.7 %copy-start.8 = (f32[8,10]{1,0:T(8,128)S(1)}, f32[8,10]{1,0:T(8,128)}, u32[]{:S(2)}) copy-start(f32[8,10]{1,0:T(8,128)} %cpl.1) | copy-start | bytes 964
  8.4 0.7 %copy-start.9 = (f32[8,128]{1,0:T(8,128)S(1)}, f32[8,128]{1,0:T(8,128)}, u32[]{:S(2)}) copy-start(f32[8,128]{1,0:T(8,128)} %rel.1) | copy-start | bytes 12292
  9.0 0.7 %copy-start.10 = (s32[1,1,64,1]{2,3,1,0:T(1,128)S(1)}, s32[1,1,64,1]{2,3,1,0:T(1,128)}, u32[]{:S(2)}) copy-start(s32[1,1,64,1]{2,3,1,0:T(1,128)} %param.14) | copy-start | bytes 772

commit v3 on v2

v3 whole, which is shorter than its diff:
```python
import functools

import jax
import jax.numpy as jnp
import numpy as np
from jax import lax
from jax.experimental import pallas as pl
from jax.experimental.pallas import tpu as pltpu
from jax.sharding import PartitionSpec as P

f32 = jnp.float32
bf16 = jnp.bfloat16
MESH = pl.DeviceIdType.MESH
HBM = pl.BlockSpec(memory_space=pltpu.HBM)
VMEM = pl.BlockSpec(memory_space=pltpu.VMEM)
SMEM = pl.BlockSpec(memory_space=pltpu.SMEM)

NF, NTEND, LEV = 10, 8, 128
PAIRS = NF // 2
XROWS, YROWS = 16, 32
BLOCKS = XROWS // 4
NODES = 4 * YROWS
CELLS = YROWS
CX, CZ, CY = 4, 8, 4
DT_DYN, DT_PHY = 0.1, 0.25


def gll_matrix():
    points = np.array([-1.0, -1.0 / np.sqrt(5.0), 1.0 / np.sqrt(5.0), 1.0])
    bary = np.ones(4)
    for i in range(4):
        for j in range(4):
            if i != j:
                bary[i] /= points[i] - points[j]
    matrix = np.zeros((4, 4))
    for i in range(4):
        for j in range(4):
            if i != j:
                matrix[i, j] = bary[j] / bary[i] / (points[i] - points[j])
        matrix[i, i] = -np.sum(matrix[i])
    return matrix


def constants():
    d = gll_matrix()
    weight1 = np.array([0.5, 1.0, 1.0, 0.5])
    weight = np.kron(weight1, np.tile(weight1, YROWS // 4))
    along_x = np.kron(d, np.eye(YROWS))
    along_y = np.kron(np.eye(4 * YROWS // 4), d)
    both = np.concatenate([along_x, along_y]) * (-DT_DYN * np.tile(weight, 2))[:, None]
    high = np.asarray(both, np.float32).astype(jnp.bfloat16)
    low = (both - high.astype(np.float64)).astype(np.float32).astype(jnp.bfloat16)
    derive = np.concatenate([high, low], axis=1)
    share = np.eye(YROWS)
    for y in range(3, YROWS - 1, 4):
        share[y, y + 1] = share[y + 1, y] = 1.0
    advance = np.concatenate([np.kron(np.eye(4), share), np.eye(NODES)], axis=1)
    edges = np.zeros((BLOCKS, NODES, 2 * XROWS))
    for block in range(BLOCKS):
        for i in range(4):
            edges[block, i * YROWS, 4 * block + i] = 1.0
            edges[block, i * YROWS + YROWS - 1, XROWS + 4 * block + i] = 1.0
    return derive, advance.astype(jnp.bfloat16), edges.astype(jnp.bfloat16)


def iota(shape, dim):
    return lax.broadcasted_iota(jnp.int32, shape, dim)


def halves(x):
    high = x.astype(bf16)
    return high, (x - high.astype(f32)).astype(bf16)


def mm(a, b):
    return jnp.dot(a, b, preferred_element_type=f32)


def mm_nt(a, b):
    return lax.dot_general(a, b, (((1,), (1,)), ((), ())), preferred_element_type=f32)


def mm2(a, b):
    high, low = halves(b)
    return mm(a, high) + mm(a, low)


def main_kernel(
    sec, tc, tn, own, frc, vmap, cpl, rel, derive_h, advance_h, edges_h,
    packed, landed,
    cur, start, adv, advx, advd, wind, xlo, xhi, yrow, ysend, ylo, yhi, halo, csend, clo, chi,
    tc_v, tn_v, own_v, frc_v, v_v, rel_v, cpl_v, derive, advance, edges,
    f2, ts, win, wout, vv, fa, fb1, fs2, fb2, fbc, cells, split, mixed, act, base, tend,
    small_sem, q_sem, s_send, s_recv, e_send, e_recv, c_send, c_recv, f_send, f_recv,
    o_send, o_recv,
):
    m, gx, gy = lax.axis_index("grp"), lax.axis_index("gx"), lax.axis_index("gy")
    z, x = gx // CX, gx % CX
    ngx = CX * CZ
    other = 1 - m
    partner = (other, gx, gy)
    left, right = (gx + ngx - 1) % ngx, (gx + 1) % ngx
    down, up = (gy + CY - 1) % CY, (gy + 1) % CY

    def plane_peer(j):
        return (1, z * CX + (x + j // CY) % CX, (gy + j % CY) % CY)

    def line_peer(member, j):
        return (member, ((z + j) % CZ) * CX + x, gy)

    barrier = pltpu.get_barrier_semaphore()

    def greet(peers):
        for peer in peers:
            pl.semaphore_signal(barrier, inc=1, device_id=peer, device_id_type=MESH)

    @pl.when(m == 0)
    def _():
        greet([partner, (0, left, gy), (0, gx, down), (0, gx, up), (0, left, down), (0, left, up)])
        greet([line_peer(1, j) for j in range(1, CZ)])

    @pl.when(m == 1)
    def _():
        greet([partner, (0, right, gy), (0, gx, down), (0, gx, up), (0, right, down), (0, right, up)])
        greet([plane_peer(j) for j in range(1, CX * CY)])
        greet([line_peer(1, j) for j in range(1, CZ)])

    small = [
        pltpu.make_async_copy(src, dst, small_sem.at[k])
        for k, (src, dst) in enumerate([
            (frc, frc_v), (derive_h, derive), (advance_h, advance), (edges_h, edges),
            (tc.at[pl.ds(m * BLOCKS, BLOCKS)], tc_v), (tn.at[pl.ds(m * BLOCKS, BLOCKS)], tn_v),
            (own, own_v), (vmap, v_v), (rel, rel_v), (cpl, cpl_v),
        ])
    ]

    def current_in(p):
        fields = pl.ds(2 * p, 2)
        return pltpu.make_async_copy(sec.at[0, fields], cur.at[fields], q_sem.at[p])

    def start_in(p):
        fields = pl.ds(2 * p, 2)
        return pltpu.make_async_copy(
            sec.at[0, fields, pl.ds(XROWS, XROWS)], start.at[fields], s_recv.at[p]
        )

    def start_out(p):
        fields = pl.ds(2 * p, 2)
        return pltpu.make_async_remote_copy(
            sec.at[0, fields, pl.ds(0, XROWS)], start.at[fields], s_send.at[p], s_recv.at[p],
            device_id=partner, device_id_type=MESH,
        )

    def start_wait(p):
        fields = start.at[pl.ds(2 * p, 2)]
        pltpu.make_async_copy(fields, fields, s_recv.at[p]).wait()

    def edge_copies(p, kinds=range(7)):
        fields = pl.ds(2 * p, 2)
        return [
            pltpu.make_async_remote_copy(
                src, dst, e_send.at[k, p], e_recv.at[k, p], device_id=to, device_id_type=MESH
            )
            for k, (src, dst, to) in enumerate([
                (advx.at[fields], adv.at[fields], (1, gx, gy)),
                (adv.at[fields, 0], xhi.at[fields], (1, left, gy)),
                (advx.at[fields, XROWS - 1], xlo.at[fields], (0, right, gy)),
                (ysend.at[0, 0, fields], yhi.at[fields], (0, gx, down)),
                (ysend.at[0, 1, fields], yhi.at[fields], (1, gx, down)),
                (ysend.at[1, 0, fields], ylo.at[fields], (0, gx, up)),
                (ysend.at[1, 1, fields], ylo.at[fields], (1, gx, up)),
            ])
            if k in kinds
        ]

    def corner_copies(sides=(0, 1)):
        return [
            pltpu.make_async_remote_copy(
                csend.at[2 * xs + ys], (chi, clo)[xs].at[1 - ys], c_send.at[2 * xs + ys],
                c_recv.at[2 * xs + ys],
                device_id=(1 - xs, (left, right)[xs], (down, up)[ys]), device_id_type=MESH,
            )
            for xs in sides for ys in range(2)
        ]

    def plane_copy(j, arriving):
        _, tx, ty = plane_peer(j)
        to = (tx % CX) * CY + ty
        me = x * CY + gy
        if arriving:
            me = ((x + CX - j // CY) % CX) * CY + (gy + CY - j % CY) % CY
        return pltpu.make_async_remote_copy(
            fa.at[pl.ds(pl.multiple_of(to * 8, 8), 8)],
            fb1.at[pl.ds(pl.multiple_of(me * 8, 8), 8)],
            f_send.at[0, j], f_recv.at[0, j], device_id=plane_peer(j), device_id_type=MESH,
        )

    def line_copy(member, j, arriving=False):
        to, me = (z + j) % CZ, z
        if arriving:
            me = (z + CZ - j) % CZ
        return pltpu.make_async_remote_copy(
            fs2.at[pl.ds(pl.multiple_of(to * 16, 16), 16)],
            fb2.at[pl.ds(pl.multiple_of(me * 16, 16), 16)],
            f_send.at[1 + member, j], f_recv.at[1, j],
            device_id=line_peer(member, j), device_id_type=MESH,
        )

    @pl.when(m == 0)
    def _():
        for p in range(PAIRS):
            current_in(p).start()
        for copy in small:
            copy.start()
        small[1].wait()

        def put(p, row, value, raw):
            for k in range(2):
                part = value[:, k * LEV:(k + 1) * LEV]
                f = 2 * p + k
                if row < XROWS:
                    adv[f, row] = part.astype(bf16)
                else:
                    advx[f, row - XROWS] = part.astype(bf16)
                for side, edge in ((0, 0), (1, YROWS - 1)):
                    line = part[edge:edge + 1, :]
                    yrow[side, f, row:row + 1, :] = line
                    if raw is not None:
                        csend[2 * raw + side, f:f + 1, :] = line

        for p in range(PAIRS):
            current_in(p).wait()
            if p == 0:
                for k in range(2):
                    for block in range(2 * BLOCKS):
                        rows = cur[k, 4 * block:4 * block + 4].reshape(NODES, LEV)
                        wind[k, block] = rows.astype(f32)
            last = None
            for block in range(2 * BLOCKS):
                pair = [
                    cur[2 * p + k, 4 * block:4 * block + 4].reshape(NODES, LEV) for k in range(2)
                ]
                once = jnp.concatenate(pair, axis=1)
                slopes = mm(derive[...], jnp.concatenate([once, once], axis=0))
                u, v = wind[0, block], wind[1, block]
                value = jnp.concatenate([u, u], axis=1) * slopes[:NODES]
                value = value + jnp.concatenate([v, v], axis=1) * slopes[NODES:]
                first = value[:YROWS]
                if block == 0:
                    put(p, 0, first, 0)
                else:
                    shared = last + first
                    put(p, 4 * block - 1, shared, None)
                    put(p, 4 * block, shared, None)
                put(p, 4 * block + 1, value[YROWS:2 * YROWS], None)
                put(p, 4 * block + 2, value[2 * YROWS:3 * YROWS], None)
                last = value[3 * YROWS:]
            put(p, 2 * XROWS - 1, last, 1)
            for side in range(2):
                for k in range(2):
                    f = 2 * p + k
                    for half in range(2):
                        lines = yrow[side, f, half * XROWS:(half + 1) * XROWS]
                        ysend[side, half, f] = lines.astype(bf16)
            if p == SENT:
                pl.semaphore_wait(barrier, 11)
                for q in range(p):
                    for copy in edge_copies(q):
                        copy.start()
            if p >= SENT:
                for copy in edge_copies(p):
                    copy.start()
        for copy in corner_copies():
            copy.start()
        xhi[...] = jnp.zeros_like(xhi)
        chi[...] = jnp.zeros_like(chi)

    @pl.when(m == 1)
    def _():
        for p in range(PAIRS):
            start_in(p).start()
        for copy in small:
            copy.start()
        small[0].wait()
        for g in range(NTEND):
            f2[4 * g:4 * g + 4, :] = frc_v[g]
        source = iota((128, 256), 0)
        source = 2 * ((source % CZ) * (CX * CY) + source // CZ)
        slot = iota((128, 256), 1)
        rows_high, rows_low = halves(f2[...])
        empty = jnp.zeros((32, 256), bf16)
        total = jnp.zeros((128, 128), f32)
        for r in range(2):
            pick = (slot == source + r).astype(f32).astype(bf16)
            for part in (rows_high, rows_low):
                stack = [empty] * 4
                stack[r] = part
                total = total + mm_nt(pick, jnp.concatenate(stack, axis=0))
        fa[...] = total
        xlo[...] = jnp.zeros_like(xlo)
        clo[...] = jnp.zeros_like(clo)
        pl.semaphore_wait(barrier, 30)
        for j in range(1, CX * CY):
            plane_copy(j, False).start()
        for p in range(PAIRS):
            start_out(p).start()
        mine = pl.ds(pl.multiple_of((x * CY + gy) * 8, 8), 8)
        fb1[mine, :] = fa[mine, :]

    for copy in small[4:]:
        copy.wait()
    spread = (iota((16, 128), 0) == (iota((16, 128), 1) // 32) * 4 + iota((16, 128), 1) % 4)
    spread = spread.astype(f32).astype(bf16)
    inside = (iota((128, 128), 0) // 4) % 8 == (iota((128, 128), 1) // 4) % 8
    for k, ref in enumerate((tc_v, tn_v)):
        for block in range(BLOCKS):
            for ey in range(8):
                row = block * 32 + ey * 4
                ts[row:row + 4, :] = ref[block, ey].astype(f32)
        wide = jnp.where(inside, mm(ts[...].astype(bf16), spread), 0.0)
        if k == 0:
            win[...] = wide.astype(bf16)
        else:
            turned = jnp.transpose(wide * DT_PHY)
            eye = (iota((128, 128), 0) == iota((128, 128), 1)).astype(f32).astype(bf16)
            for block in range(BLOCKS):
                moved = turned if block == 0 else pltpu.roll(turned, 128 - 32 * block, 1)
                wout[block, :, 0:128] = eye
                wout[block, :, 128:256] = moved.astype(bf16)
    v_high, v_low = halves(v_v[...])
    vv[0:128, 0:128] = v_high
    vv[128:256, 0:128] = v_high
    vv[0:128, 128:256] = v_low
    vv[128:256, 128:256] = jnp.zeros((128, 128), bf16)

    owned = (iota((128, 64), 0) == own_v[...]).astype(f32)
    before = (iota((64, 64), 0) < iota((64, 64), 1)).astype(f32).astype(bf16)
    rank = mm(owned.astype(bf16), before)
    mine = (iota((128, 64), 1) == m * 32 + iota((128, 64), 0) // 4).astype(f32).astype(bf16)
    from0 = mm_nt(mine, jnp.where(rank < 0.5, owned, 0.0).astype(bf16)).astype(bf16)
    from1 = mm_nt(mine, jnp.where(rank < 0.5, 0.0, owned).astype(bf16)).astype(bf16)

    @pl.when(m == 0)
    def _():
        small[2].wait()
        small[3].wait()
        small[0].wait()
        for p in range(PAIRS):
            for copy in edge_copies(p, (2, 3, 5)):
                copy.wait_recv()
        for copy in corner_copies((1,)):
            copy.wait_recv()

    @pl.when(m == 1)
    def _():
        small[1].wait()
        small[2].wait()
        small[3].wait()
        for j in range(1, CX * CY):
            plane_copy(j, True).wait_recv()
        for k in range(CZ):
            fs2[16 * k:16 * k + 16, :] = fb1[pl.ds(k, 16, stride=CZ), :]
        for j in range(1, CZ):
            for member in range(2):
                line_copy(member, j).start()
        mine = pl.ds(pl.multiple_of(z * 16, 16), 16)
        pltpu.make_async_remote_copy(
            fs2.at[mine], fb2.at[mine], f_send.at[1, 0], f_recv.at[1, 0],
            device_id=partner, device_id_type=MESH,
        ).start()
        fb2[mine, :] = fs2[mine, :]
        for p in range(PAIRS):
            for copy in edge_copies(p, (0, 1, 4, 6)):
                copy.wait_recv()
        for copy in corner_copies((0,)):
            copy.wait_recv()

    for p in range(PAIRS):
        start_wait(p)
    at = iota((XROWS, LEV), 0)
    for f in range(NF):
        for side, ref in ((0, ylo), (1, yhi)):
            first = jnp.broadcast_to(clo[side, f:f + 1, :], (XROWS, LEV))
            final = jnp.broadcast_to(chi[side, f:f + 1, :], (XROWS, LEV))
            value = ref[f].astype(f32)
            value = value + jnp.where(at == 0, first, jnp.where(at == XROWS - 1, final, 0.0))
            halo[f, side * XROWS:(side + 1) * XROWS, :] = value.astype(bf16)

    for block in range(BLOCKS):
        weights = win[32 * block:32 * block + 32, :]
        for p in range(PAIRS):
            parts, starts = [], []
            for k in range(2):
                f = 2 * p + k
                rows = [adv[f, 4 * block + i] for i in range(4)]
                if block == 0:
                    rows[0] = (rows[0].astype(f32) + xlo[f].astype(f32)).astype(bf16)
                if block == BLOCKS - 1:
                    rows[3] = (rows[3].astype(f32) + xhi[f].astype(f32)).astype(bf16)
                begun = start[f, 4 * block:4 * block + 4].reshape(NODES, LEV)
                parts.append(jnp.concatenate(rows + [begun], axis=0))
                starts.append(halo[f])
            value = mm(advance[...], jnp.concatenate(parts, axis=1))
            value = value + mm(edges[block], jnp.concatenate(starts, axis=1))
            value = value.astype(bf16)
            got = mm(weights, value)
            for k in range(2):
                f = 2 * p + k
                advd[f, block] = value[:, k * LEV:(k + 1) * LEV]
                one = got[:, k * LEV:(k + 1) * LEV]
                cells[block, f] = one
                high, low = halves(one)
                split[block, f, :, 0:LEV] = high
                split[block, f, :, LEV:2 * LEV] = low
        for p in range(PAIRS):
            lhs = split[block, 2 * p:2 * p + 2].reshape(2 * CELLS, 2 * LEV)
            got = mm(lhs, vv[...])
            got = got[:, :LEV] + got[:, LEV:]
            warm = jnp.tanh(got)
            for k in range(2):
                mixed[block, 2 * p + k] = got[k * CELLS:(k + 1) * CELLS]
                act[block, 2 * p + k] = warm[k * CELLS:(k + 1) * CELLS]
        for g in range(NTEND):
            acc = rel_v[g:g + 1, :] * (mixed[block, g] - cells[block, g])
            for f in range(NF):
                acc = acc + cpl_v[g, f] * act[block, f]
            base[block, g] = acc

    @pl.when(m == 0)
    def _():
        for j in range(CZ):
            line_copy(0, j, True).wait_recv()

    @pl.when(m == 1)
    def _():
        for j in range(1, CZ):
            line_copy(1, j, True).wait_recv()

    table = fb2[...]
    lines = mm2(from0, table) + mm2(from1, pltpu.roll(table, 96, 1))
    lane = iota((128, 128), 1)
    lines = jnp.where((lane < 32) & (lane % 4 == iota((128, 128), 0) % 4), lines, 0.0)
    high = lines.astype(bf16).astype(f32)
    lines = (high + pltpu.roll(lines - high, 32, 1)).astype(bf16)
    group = jnp.where(iota((128, 128), 0) < 64, (iota((128, 128), 0) // 4) % 8, 8)
    for g in range(NTEND):
        fbc[g] = mm(lines, (group == g).astype(f32).astype(bf16))

    lower = iota((YROWS, LEV), 1) < LEV // 2

    def pack(block, f, value):
        for i in range(2):
            a = value[i * YROWS:(i + 1) * YROWS]
            b = value[(i + 2) * YROWS:(i + 3) * YROWS]
            packed[0, block, f, i] = jnp.where(lower, a, pltpu.roll(b, 64, 1)).astype(bf16)
            packed[1, block, f, i] = jnp.where(lower, pltpu.roll(a, 64, 1), b).astype(bf16)

    def out_copy(block):
        return pltpu.make_async_remote_copy(
            packed.at[other, block], landed.at[block], o_send.at[block], o_recv.at[block],
            device_id=partner, device_id_type=MESH,
        )

    for block in range(BLOCKS):
        for f in range(NTEND, NF):
            pack(block, f, advd[f, block].astype(f32))
        for g in range(NTEND):
            tend[block, g] = (base[block, g] + fbc[g, 32 * block:32 * block + 32, :]).astype(bf16)
        for p in range(NTEND // 2):
            parts = [
                jnp.concatenate([advd[2 * p + k, block], tend[block, 2 * p + k]], axis=0)
                for k in range(2)
            ]
            value = mm(wout[block, :, 0:NODES + CELLS], jnp.concatenate(parts, axis=1))
            for k in range(2):
                pack(block, 2 * p + k, value[:, k * LEV:(k + 1) * LEV])
        out_copy(block).start()

    @pl.when(m == 0)
    def _():
        for p in range(PAIRS):
            for copy in edge_copies(p):
                copy.wait_send()
        for copy in corner_copies():
            copy.wait_send()

    @pl.when(m == 1)
    def _():
        for p in range(PAIRS):
            start_out(p).wait_send()
        for j in range(1, CX * CY):
            plane_copy(j, False).wait_send()
        for j in range(1, CZ):
            for member in range(2):
                line_copy(member, j).wait_send()
        line_copy(0, 0).wait_send()

    for block in range(BLOCKS):
        out_copy(block).wait_send()
        out_copy(block).wait_recv()


SENT = 1


def main_call(args):
    v = pltpu.VMEM
    packed_shape = (BLOCKS, NF, 2, YROWS, LEV)
    dma = pltpu.SemaphoreType.DMA
    scratch = [
        v((NF, 2 * XROWS, YROWS, LEV), bf16),
        v((NF, XROWS, YROWS, LEV), bf16),
        v((NF, XROWS, YROWS, LEV), bf16),
        v((NF, XROWS, YROWS, LEV), bf16),
        v((NF, BLOCKS, NODES, LEV), bf16),
        v((2, 2 * BLOCKS, NODES, LEV), f32),
        v((NF, YROWS, LEV), bf16),
        v((NF, YROWS, LEV), bf16),
        v((2, NF, 2 * XROWS, LEV), f32),
        v((2, 2, NF, XROWS, LEV), bf16),
        v((NF, XROWS, LEV), bf16),
        v((NF, XROWS, LEV), bf16),
        v((NF, 2 * XROWS, LEV), bf16),
        v((4, 16, LEV), f32),
        v((2, 16, LEV), f32),
        v((2, 16, LEV), f32),
        v((BLOCKS, 8, 4, 16), bf16),
        v((BLOCKS, 8, 4, 16), bf16),
        v((1, 64), jnp.int32),
        v((NTEND, 4, 256), f32),
        v((LEV, LEV), f32),
        v((NTEND, LEV), f32),
        pltpu.SMEM((NTEND, NF), f32),
        v((2 * NODES, 2 * NODES), bf16),
        v((NODES, 2 * NODES), bf16),
        v((BLOCKS, NODES, 2 * XROWS), bf16),
        v((32, 256), f32),
        v((128, 16), f32),
        v((128, 128), bf16),
        v((BLOCKS, 128, 256), bf16),
        v((256, 256), bf16),
    ]
    scratch += [v((128, 128), f32)] * 4
    scratch += [
        v((NTEND, 128, LEV), f32),
        v((BLOCKS, NF, CELLS, LEV), f32),
        v((BLOCKS, NF, CELLS, 2 * LEV), bf16),
        v((BLOCKS, NF, CELLS, LEV), f32),
        v((BLOCKS, NF, CELLS, LEV), f32),
        v((BLOCKS, NTEND, CELLS, LEV), f32),
        v((BLOCKS, NTEND, CELLS, LEV), bf16),
        dma((10,)), dma((PAIRS,)), dma((PAIRS,)), dma((PAIRS,)),
        dma((7, PAIRS)), dma((7, PAIRS)), dma((4,)), dma((4,)),
        dma((3, CX * CY)), dma((2, CX * CY)), dma((BLOCKS,)), dma((BLOCKS,)),
    ]
    return pl.pallas_call(
        main_kernel,
        out_shape=(
            jax.ShapeDtypeStruct((2,) + packed_shape, bf16),
            jax.ShapeDtypeStruct(packed_shape, bf16),
        ),
        in_specs=[HBM] * 11,
        out_specs=(VMEM, VMEM),
        scratch_shapes=scratch,
        compiler_params=pltpu.CompilerParams(
            collective_id=0, has_side_effects=True, vmem_limit_bytes=40 * 2**20
        ),
    )(*args)


def unpack_kernel(packed, landed, out, stage, sems):
    m = lax.axis_index("grp")

    def copy(k, block):
        rows = (m if k == 0 else 1 - m) * XROWS + 4 * block
        return pltpu.make_async_copy(
            stage.at[k, block], out.at[:, pl.ds(rows, 4)], sems.at[k, block]
        )

    for k in range(2):
        for block in range(BLOCKS):

            def one(f):
                for i in range(2):
                    line = packed[m, block, f, i] if k == 0 else landed[block, f, i]
                    stage[k, block, f, i] = line[:, :LEV // 2]
                    moved = pltpu.roll(line.astype(f32), 64, 1).astype(bf16)
                    stage[k, block, f, i + 2] = moved[:, :LEV // 2]

            for step in range(NF):
                one(step)
            copy(k, block).start()
    for k in range(2):
        for block in range(BLOCKS):
            copy(k, block).wait()


def unpack_call(packed, landed):
    return pl.pallas_call(
        unpack_kernel,
        out_shape=jax.ShapeDtypeStruct((NF, 2 * XROWS, YROWS, LEV // 2), bf16),
        in_specs=[VMEM, VMEM],
        out_specs=HBM,
        scratch_shapes=[
            pltpu.VMEM((2, BLOCKS, NF, 4, YROWS, LEV // 2), bf16),
            pltpu.SemaphoreType.DMA((2, BLOCKS)),
        ],
        compiler_params=pltpu.CompilerParams(vmem_limit_bytes=24 * 2**20),
    )(packed, landed)


def shards(
    section_levels, to_cells, to_nodes, owner_map, forcing, vertical_map, coupling, relaxation
):
    derive, advance, edges = (jnp.asarray(c) for c in constants())
    operands = (
        section_levels, to_cells, jnp.swapaxes(to_nodes, 2, 3), owner_map.reshape(1, 64),
        forcing[0, 0], vertical_map, coupling, relaxation, derive, advance, edges,
    )
    packed, landed = main_call([
        pltpu.with_memory_space_constraint(x, pltpu.HBM) for x in operands
    ])
    return unpack_call(packed, landed)


def solution(mesh):
    in_specs = (
        P("grp", None, "gx", "gy", None),
        P("gx", "gy", None, None),
        P("gx", "gy", None, None),
        P("gx", "gy", None, None),
        P("gx", "gy", None, None, None),
        P(),
        P(),
        P(),
    )
    out_specs = P(None, "gx", "gy", "grp")
    return jax.shard_map(shards, mesh=mesh, in_specs=in_specs, out_specs=out_specs, check_vma=False)
```

time: 49.7 us -> 27.7 us (0.56)
  Pallas kernels: 39.5 us -> 27.6 us
  local copies, waits for them, and re-layouts: 9.69 us -> 0 us
    pallas_call x1, Pallas kernels: 37.8 us -> 26 us  [main_call(): pl.pallas_call(main_kernel, out_shape=(jax.ShapeDtypeStruct((2,) + packed...]
    unnamed x22 -> x0, local copies, waits for them, and re-layouts: 9.69 us -> none
where the time goes in v3:
time: 27.7 us; the launch traced here: 27.6 us
  Pallas kernels  27.6 us (100%)
    pallas_call x1, Pallas kernels, main_call(): pl.pallas_call(main_kernel, out_shape=(jax.ShapeDtypeStruct((2,) + packed...  26 us
    pallas_call x1, Pallas kernels, unpack_call(): pl.pallas_call(unpack_kernel, out_shape=jax.ShapeDtypeStruct((NF, 2 * XRO...  1.67 us

profile of v3, /device:TPU:1, one launch (start us, length us, event | category | flops | bytes accessed | tf_op | source)
XLA Modules:
  0.0 27.6 jit_solution(14651873353158252980)
XLA Ops:
  0.0 26.0 %shard_map.109 = (bf16[2,4,10,2,32,128]{5,4,3,2,1,0:T(8,128)(2,1)S(1)}, bf16[4,10,2,32,128]{4,3,2,1,0:T(8,128)(2,1)S(1)}) custom-call(bf16[1,10,32,32,128]{4,3,2,1,0:T(8,128)(2,1)} %sec.1, bf16[8,8,4,16]{3,2,1,0:T(4,128)(2,1)} %tc.1, bf16[8,8,4,16]{3,2,1,0:T(4,128)(2,1)} %bitcast.3, s32[1,64]{1,0:T(1,128)} %bitcast.5, f32[8,4,256]{2,1,0:T(4,128)} %bitcast.4, ...), custom_call_target="tpu_custom_call" | custom-call | tf_op jit(solution)/shard_map/pallas_call | solution.py:556
  26.0 1.7 %shard_map.110 = bf16[10,32,32,64]{3,2,1,0:T(8,128)(2,1)} custom-call(bf16[2,4,10,2,32,128]{5,4,3,2,1,0:T(8,128)(2,1)S(1)} %get-tuple-element.7.packed, bf16[4,10,2,32,128]{4,3,2,1,0:T(8,128)(2,1)S(1)} %get-tuple-element.8.landed), custom_call_target="tpu_custom_call" | custom-call | tf_op jit(solution)/shard_map/pallas_call | solution.py:599

commit v4 on v3

v4 whole, which is shorter than its diff:
```python
import functools

import jax
import jax.numpy as jnp
import numpy as np
from jax import lax
from jax.experimental import pallas as pl
from jax.experimental.pallas import tpu as pltpu
from jax.sharding import PartitionSpec as P

f32 = jnp.float32
bf16 = jnp.bfloat16
MESH = pl.DeviceIdType.MESH
HBM = pl.BlockSpec(memory_space=pltpu.HBM)
VMEM = pl.BlockSpec(memory_space=pltpu.VMEM)
SMEM = pl.BlockSpec(memory_space=pltpu.SMEM)

NF, NTEND, LEV = 10, 8, 128
PAIRS = NF // 2
XROWS, YROWS = 16, 32
BLOCKS = XROWS // 4
NODES = 4 * YROWS
CELLS = YROWS
CX, CZ, CY = 4, 8, 4
DT_DYN, DT_PHY = 0.1, 0.25


def gll_matrix():
    points = np.array([-1.0, -1.0 / np.sqrt(5.0), 1.0 / np.sqrt(5.0), 1.0])
    bary = np.ones(4)
    for i in range(4):
        for j in range(4):
            if i != j:
                bary[i] /= points[i] - points[j]
    matrix = np.zeros((4, 4))
    for i in range(4):
        for j in range(4):
            if i != j:
                matrix[i, j] = bary[j] / bary[i] / (points[i] - points[j])
        matrix[i, i] = -np.sum(matrix[i])
    return matrix


def constants():
    d = gll_matrix()
    weight1 = np.array([0.5, 1.0, 1.0, 0.5])
    weight = np.kron(weight1, np.tile(weight1, YROWS // 4))
    along_x = np.kron(d, np.eye(YROWS))
    along_y = np.kron(np.eye(4 * YROWS // 4), d)
    both = np.concatenate([along_x, along_y]) * (-DT_DYN * np.tile(weight, 2))[:, None]
    high = np.asarray(both, np.float32).astype(jnp.bfloat16)
    low = (both - high.astype(np.float64)).astype(np.float32).astype(jnp.bfloat16)
    derive = np.concatenate([high, low], axis=1)
    share = np.eye(YROWS)
    for y in range(3, YROWS - 1, 4):
        share[y, y + 1] = share[y + 1, y] = 1.0
    advance = np.zeros((BLOCKS, NODES, NODES + 2 * XROWS))
    for block in range(BLOCKS):
        advance[block, :, :NODES] = np.kron(np.eye(4), share)
        for i in range(4):
            advance[block, i * YROWS, NODES + 4 * block + i] = 1.0
            advance[block, i * YROWS + YROWS - 1, NODES + XROWS + 4 * block + i] = 1.0
    return derive, advance.astype(jnp.bfloat16)


def iota(shape, dim):
    return lax.broadcasted_iota(jnp.int32, shape, dim)


def halves(x):
    high = x.astype(bf16)
    return high, (x - high.astype(f32)).astype(bf16)


def mm(a, b):
    return jnp.dot(a, b, preferred_element_type=f32)


def mm_nt(a, b):
    return lax.dot_general(a, b, (((1,), (1,)), ((), ())), preferred_element_type=f32)


def mm2(a, b):
    high, low = halves(b)
    return mm(a, high) + mm(a, low)


def main_kernel(
    sec, tc, tn, own, frc, vmap, cpl, rel, derive_h, advance_h,
    packed, landed, given, chosen,
    cur, start, adv, advx, advd, wind, xfirst, xlast, xlo, xhi, yrow, ysend, ylo, yhi,
    csend, cgot, clo, chi, raw_first, raw_last,
    tc_v, tn_v, own_v, frc_v, v_v, rel_v, cpl_v, derive, advance,
    f2, ts, win, wgiven, vv, fa, fb1, fs2, fb2, cells, split, mixed, act, tend,
    small_sem, q_sem, s_send, s_recv, e_send, e_recv, c_send, c_recv, f_send, f_recv,
    o_send, o_recv,
):
    m, gx, gy = lax.axis_index("grp"), lax.axis_index("gx"), lax.axis_index("gy")
    z, x = gx // CX, gx % CX
    ngx = CX * CZ
    other = 1 - m
    partner = (other, gx, gy)
    left, right = (gx + ngx - 1) % ngx, (gx + 1) % ngx
    down, up = (gy + CY - 1) % CY, (gy + 1) % CY

    def plane_peer(j):
        return (1, z * CX + (x + j // CY) % CX, (gy + j % CY) % CY)

    def line_peer(member, j):
        return (member, ((z + j) % CZ) * CX + x, gy)

    barrier = pltpu.get_barrier_semaphore()

    def greet(peers):
        for peer in peers:
            pl.semaphore_signal(barrier, inc=1, device_id=peer, device_id_type=MESH)

    small = [
        pltpu.make_async_copy(src, dst, small_sem.at[k])
        for k, (src, dst) in enumerate([
            (frc, frc_v), (derive_h, derive), (advance_h, advance),
            (tc.at[pl.ds(m * BLOCKS, BLOCKS)], tc_v), (tn, tn_v),
            (own, own_v), (vmap, v_v), (rel, rel_v), (cpl, cpl_v),
        ])
    ]

    def current_in(block):
        rows = pl.ds(4 * block, 4)
        return pltpu.make_async_copy(sec.at[0, :, rows], cur.at[:, rows], q_sem.at[block])

    def row_of(member, turn):
        return (1 - member) * (BLOCKS - 1 - turn) + member * turn

    def start_in(turn):
        return pltpu.make_async_copy(
            sec.at[0, :, pl.ds(XROWS + 4 * turn, 4)], start.at[:, pl.ds(4 * turn, 4)],
            s_recv.at[turn],
        )

    def start_out(turn):
        rows = pl.ds(4 * (BLOCKS - 1 - turn), 4)
        return pltpu.make_async_remote_copy(
            sec.at[0, :, rows], start.at[:, rows], s_send.at[turn], s_recv.at[turn],
            device_id=partner, device_id_type=MESH,
        )

    def start_wait(turn):
        rows = start.at[:, pl.ds(4 * row_of(m, turn), 4)]
        pltpu.make_async_copy(rows, rows, s_recv.at[turn]).wait()

    def edge_copies(kinds):
        plan = [
            (adv.at[:, 0], xfirst, partner),
            (advx.at[:, XROWS - 1], xlast, partner),
            (csend, cgot, partner),
            (ysend.at[0, 0], yhi, (0, gx, down)),
            (ysend.at[0, 1], yhi, (1, gx, down)),
            (ysend.at[1, 0], ylo, (0, gx, up)),
            (ysend.at[1, 1], ylo, (1, gx, up)),
            (xfirst, xhi, (1, left, gy)),
            (xlast, xlo, (0, right, gy)),
        ]
        for block in range(BLOCKS):
            rows = pl.ds(4 * block, 4)
            plan.append((advx.at[:, rows], adv.at[:, rows], partner))
        return [
            pltpu.make_async_remote_copy(
                plan[k][0], plan[k][1], e_send.at[k], e_recv.at[k],
                device_id=plan[k][2], device_id_type=MESH,
            )
            for k in kinds
        ]

    def corner_copies(sides=(0, 1)):
        return [
            pltpu.make_async_remote_copy(
                cgot.at[2 * xs + ys], (chi, clo)[xs].at[1 - ys], c_send.at[2 * xs + ys],
                c_recv.at[2 * xs + ys],
                device_id=(1 - xs, (left, right)[xs], (down, up)[ys]), device_id_type=MESH,
            )
            for xs in sides for ys in range(2)
        ]

    def plane_copy(j, arriving):
        _, tx, ty = plane_peer(j)
        to = (tx % CX) * CY + ty
        me = x * CY + gy
        if arriving:
            me = ((x + CX - j // CY) % CX) * CY + (gy + CY - j % CY) % CY
        return pltpu.make_async_remote_copy(
            fa.at[pl.ds(pl.multiple_of(to * 8, 8), 8)],
            fb1.at[pl.ds(pl.multiple_of(me * 8, 8), 8)],
            f_send.at[0, j], f_recv.at[0, j], device_id=plane_peer(j), device_id_type=MESH,
        )

    def line_copy(member, j, arriving=False):
        to, me = (z + j) % CZ, z
        if arriving:
            me = (z + CZ - j) % CZ
        return pltpu.make_async_remote_copy(
            fs2.at[pl.ds(pl.multiple_of(to * 16, 16), 16)],
            fb2.at[pl.ds(pl.multiple_of(me * 16, 16), 16)],
            f_send.at[1 + member, j], f_recv.at[1, j],
            device_id=line_peer(member, j), device_id_type=MESH,
        )

    @pl.when(m == 0)
    def _():
        small[1].start()
        for block in ROWS:
            current_in(block).start()
        greet([partner, (0, gx, down), (0, gx, up)])
        greet([(1, left, gy), (1, left, down), (1, left, up)])
        greet([line_peer(1, j) for j in range(1, CZ)])
        for k, copy in enumerate(small):
            if k != 1:
                copy.start()
        small[1].wait()

        def put(p, row, value, raw):
            for k in range(2):
                part = value[:, k * LEV:(k + 1) * LEV]
                f = 2 * p + k
                if row < XROWS:
                    adv[f, row] = part.astype(bf16)
                else:
                    advx[f, row - XROWS] = part.astype(bf16)
                for side, edge in ((0, 0), (1, YROWS - 1)):
                    line = part[edge:edge + 1, :]
                    yrow[side, f, row:row + 1, :] = line
                    if raw is not None:
                        csend[2 * raw + side, f:f + 1, :] = line

        for turn, block in enumerate(ROWS):
            current_in(block).wait()
            for k in range(2):
                wind[k, block] = cur[k, 4 * block:4 * block + 4].reshape(NODES, LEV).astype(f32)
            for p in range(PAIRS):
                pair = [
                    cur[2 * p + k, 4 * block:4 * block + 4].reshape(NODES, LEV) for k in range(2)
                ]
                once = jnp.concatenate(pair, axis=1)
                slopes = mm(derive[...], jnp.concatenate([once, once], axis=0))
                u, v = wind[0, block], wind[1, block]
                value = jnp.concatenate([u, u], axis=1) * slopes[:NODES]
                value = value + jnp.concatenate([v, v], axis=1) * slopes[NODES:]
                first, last = value[:YROWS], value[3 * YROWS:]
                if block == 0:
                    put(p, 0, first, 0)
                elif block == 2 * BLOCKS - 1:
                    raw_first[p] = first
                    put(p, 4 * block + 3, last, 1)
                else:
                    shared = raw_last[p] + first
                    put(p, 4 * block - 1, shared, None)
                    put(p, 4 * block, shared, None)
                put(p, 4 * block + 1, value[YROWS:2 * YROWS], None)
                put(p, 4 * block + 2, value[2 * YROWS:3 * YROWS], None)
                if block == 2 * BLOCKS - 2:
                    shared = last + raw_first[p]
                    put(p, 4 * block + 3, shared, None)
                    put(p, 4 * block + 4, shared, None)
                elif block < 2 * BLOCKS - 2:
                    raw_last[p] = last
            if turn == 1:
                pl.semaphore_wait(barrier, 5)
                for copy in edge_copies((0, 1, 2)):
                    copy.start()
        for f in range(NF):
            for side in range(2):
                for half in range(2):
                    lines = yrow[side, f, half * XROWS:(half + 1) * XROWS]
                    ysend[side, half, f] = lines.astype(bf16)
        for copy in edge_copies((3, 4, 5, 6, 9, 10, 11, 12)):
            copy.start()
        xhi[...] = jnp.zeros_like(xhi)
        chi[...] = jnp.zeros_like(chi)

    @pl.when(m == 1)
    def _():
        small[0].start()
        greet([partner, (0, gx, down), (0, gx, up)])
        greet([(1, right, gy), (1, right, down), (1, right, up)])
        greet([plane_peer(j) for j in range(1, CX * CY)])
        greet([line_peer(1, j) for j in range(1, CZ)])
        for turn in range(BLOCKS):
            start_in(turn).start()
        for copy in small[1:]:
            copy.start()
        small[0].wait()
        for g in range(NTEND):
            f2[4 * g:4 * g + 4, :] = frc_v[g]
        source = iota((128, 256), 0)
        source = 2 * ((source % CZ) * (CX * CY) + source // CZ)
        slot = iota((128, 256), 1)
        rows_high, rows_low = halves(f2[...])
        empty = jnp.zeros((32, 256), bf16)
        total = jnp.zeros((128, 128), f32)
        for r in range(2):
            pick = (slot == source + r).astype(f32).astype(bf16)
            for part in (rows_high, rows_low):
                stack = [empty] * 4
                stack[r] = part
                total = total + mm_nt(pick, jnp.concatenate(stack, axis=0))
        fa[...] = total
        xlo[...] = jnp.zeros_like(xlo)
        clo[...] = jnp.zeros_like(clo)
        pl.semaphore_wait(barrier, 36)
        for j in range(1, CX * CY):
            plane_copy(j, False).start()
        for turn in range(BLOCKS):
            start_out(turn).start()
        mine = pl.ds(pl.multiple_of((x * CY + gy) * 8, 8), 8)
        fb1[mine, :] = fa[mine, :]

    def relay():
        for j in range(1, CX * CY):
            plane_copy(j, True).wait_recv()
        for k in range(CZ):
            fs2[16 * k:16 * k + 16, :] = fb1[pl.ds(k, 16, stride=CZ), :]
        for j in range(1, CZ):
            for member in range(2):
                line_copy(member, j).start()
        mine = pl.ds(pl.multiple_of(z * 16, 16), 16)
        pltpu.make_async_remote_copy(
            fs2.at[mine], fb2.at[mine], f_send.at[1, 0], f_recv.at[1, 0],
            device_id=partner, device_id_type=MESH,
        ).start()
        fb2[mine, :] = fs2[mine, :]

    for copy in small[3:]:
        copy.wait()
    spread = (iota((16, 128), 0) == (iota((16, 128), 1) // 32) * 4 + iota((16, 128), 1) % 4)
    spread = spread.astype(f32).astype(bf16)
    inside = (iota((128, 128), 0) // 4) % 8 == (iota((128, 128), 1) // 4) % 8
    for k in range(3):
        for block in range(BLOCKS):
            for ey in range(8):
                row = block * 32 + ey * 4
                one = tc_v[block, ey] if k == 0 else tn_v[block + BLOCKS * (k - 1), ey]
                ts[row:row + 4, :] = one.astype(f32)
        wide = jnp.where(inside, mm(ts[...].astype(bf16), spread), 0.0)
        if k == 0:
            for block in range(BLOCKS):
                win[block] = wide[32 * block:32 * block + 32].astype(bf16)
        else:
            turned = jnp.transpose(wide * DT_PHY)
            for block in range(BLOCKS):
                moved = turned if block == 0 else pltpu.roll(turned, 128 - 32 * block, 1)
                wgiven[block + BLOCKS * (k - 1)] = moved.astype(bf16)
    v_high, v_low = halves(v_v[...])
    vv[0:128, 0:128] = v_high
    vv[128:256, 0:128] = v_high
    vv[0:128, 128:256] = v_low
    vv[128:256, 128:256] = jnp.zeros((128, 128), bf16)

    owned = (iota((128, 64), 0) == own_v[...]).astype(f32)
    before = (iota((64, 64), 0) < iota((64, 64), 1)).astype(f32).astype(bf16)
    rank = mm(owned.astype(bf16), before)
    mine = (iota((256, 64), 1) == iota((256, 64), 0) // 4).astype(f32).astype(bf16)
    from0 = mm_nt(mine, jnp.where(rank < 0.5, owned, 0.0).astype(bf16)).astype(bf16)
    from1 = mm_nt(mine, jnp.where(rank < 0.5, 0.0, owned).astype(bf16)).astype(bf16)

    for g in range(NTEND):
        k, lane = iota((128, LEV), 0), iota((128, LEV), 1)
        chosen[g] = ((k % 32 // 4 == g) & (k // 64 == lane // 64)).astype(f32).astype(bf16)

    @pl.when(m == 0)
    def _():
        small[2].wait()
        small[0].wait()
        for copy in edge_copies((3, 5)):
            copy.wait_recv()

    @pl.when(m == 1)
    def _():
        small[1].wait()
        small[2].wait()
        for copy in edge_copies((0, 1, 2)):
            copy.wait_recv()
        for copy in edge_copies((7, 8)) + corner_copies():
            copy.start()
        relay()
        for copy in edge_copies((4, 6)):
            copy.wait_recv()

    lower = iota((YROWS, LEV), 1) < LEV // 2

    def pack(block, f, value):
        for i in range(2):
            a = value[i * YROWS:(i + 1) * YROWS]
            b = value[(i + 2) * YROWS:(i + 3) * YROWS]
            packed[0, block, f, i] = jnp.where(lower, a, pltpu.roll(b, 64, 1)).astype(bf16)
            packed[1, block, f, i] = jnp.where(lower, pltpu.roll(a, 64, 1), b).astype(bf16)

    def out_copy(turn, arriving=False):
        row = row_of(m, turn)
        return pltpu.make_async_remote_copy(
            packed.at[other, row], landed.at[row_of(other, turn) if arriving else row],
            o_send.at[turn], o_recv.at[turn], device_id=partner, device_id_type=MESH,
        )

    at = iota((XROWS, LEV), 0)

    for turn in range(BLOCKS):
        row = row_of(m, turn)
        final = turn == BLOCKS - 1
        start_wait(turn)

        @pl.when(m == 0)
        def _():
            if final:
                for copy in edge_copies((8,)) + corner_copies((1,)):
                    copy.wait_recv()

        @pl.when(m == 1)
        def _():
            edge_copies((9 + turn,))[0].wait_recv()
            if final:
                for copy in edge_copies((7,)) + corner_copies((0,)):
                    copy.wait_recv()

        weights = win[row]
        for p in range(PAIRS):
            parts, begun = [], []
            for k in range(2):
                f = 2 * p + k
                rows = [adv[f, 4 * row + i] for i in range(4)]
                halo = [ylo[f], yhi[f]]
                if final:
                    rows[0] = (rows[0].astype(f32) + xlo[f].astype(f32)).astype(bf16)
                    rows[3] = (rows[3].astype(f32) + xhi[f].astype(f32)).astype(bf16)
                    for side in range(2):
                        first = jnp.broadcast_to(clo[side, f:f + 1, :], (XROWS, LEV))
                        ending = jnp.broadcast_to(chi[side, f:f + 1, :], (XROWS, LEV))
                        extra = jnp.where(at == 0, first, jnp.where(at == XROWS - 1, ending, 0.0))
                        halo[side] = (halo[side].astype(f32) + extra).astype(bf16)
                parts.append(jnp.concatenate(rows + halo, axis=0))
                begun.append(start[f, pl.ds(4 * row, 4)].reshape(NODES, LEV).astype(f32))
            value = mm(advance[row], jnp.concatenate(parts, axis=1))
            value = (value + jnp.concatenate(begun, axis=1)).astype(bf16)
            got = mm(weights, value)
            for k in range(2):
                f = 2 * p + k
                advd[f, turn] = value[:, k * LEV:(k + 1) * LEV]
                one = got[:, k * LEV:(k + 1) * LEV]
                cells[turn, f] = one
                high, low = halves(one)
                split[turn, f, :, 0:LEV] = high
                split[turn, f, :, LEV:2 * LEV] = low
        got = mm(split[turn].reshape(NF * CELLS, 2 * LEV), vv[...])
        got = got[:, :LEV] + got[:, LEV:]
        warm = jnp.tanh(got)
        for f in range(NF):
            mixed[turn, f] = got[f * CELLS:(f + 1) * CELLS]
            act[turn, f] = warm[f * CELLS:(f + 1) * CELLS]
        for g in range(NTEND):
            acc = rel_v[g:g + 1, :] * (mixed[turn, g] - cells[turn, g])
            for f in range(NF):
                acc = acc + cpl_v[g, f] * act[turn, f]
            tend[turn, g] = acc.astype(bf16)
        for f in range(NTEND, NF):
            pack(row, f, advd[f, turn].astype(f32))
        weights = wgiven[m * BLOCKS + row][:, 0:CELLS]
        for p in range(NTEND // 2):
            pair = (2 * p, 2 * p + 1)
            value = mm(weights, jnp.concatenate([tend[turn, f] for f in pair], axis=1))
            for k, f in enumerate(pair):
                pack(row, f, value[:, k * LEV:(k + 1) * LEV] + advd[f, turn].astype(f32))
        out_copy(turn).start()

    @pl.when(m == 0)
    def _():
        for j in range(CZ):
            line_copy(0, j, True).wait_recv()

    @pl.when(m == 1)
    def _():
        for j in range(1, CZ):
            line_copy(1, j, True).wait_recv()

    table = fb2[...]
    lines = mm2(from0, table) + mm2(from1, pltpu.roll(table, 96, 1))
    lane = iota((256, 128), 1)
    lines = jnp.where((lane < 32) & (lane % 4 == iota((256, 128), 0) % 4), lines, 0.0)
    lines = lines + pltpu.roll(lines, 32, 1)
    lines = lines + pltpu.roll(lines, 64, 1)
    quarter = iota((2 * YROWS, LEV), 1) // 32
    for block in range(2 * BLOCKS):
        got = mm2(wgiven[block, :, 0:32], lines[32 * block:32 * block + 32])
        both = jnp.where(quarter < 2, got[:2 * YROWS], got[2 * YROWS:])
        high = both.astype(bf16).astype(f32)
        given[block] = jnp.where(quarter % 2 == 0, high, both - high).astype(bf16)

    @pl.when(m == 0)
    def _():
        for copy in edge_copies((0, 1, 2, 3, 4, 5, 6, 9, 10, 11, 12)):
            copy.wait_send()

    @pl.when(m == 1)
    def _():
        for turn in range(BLOCKS):
            start_out(turn).wait_send()
        for copy in edge_copies((7, 8)) + corner_copies():
            copy.wait_send()
        for j in range(1, CX * CY):
            plane_copy(j, False).wait_send()
        for j in range(1, CZ):
            for member in range(2):
                line_copy(member, j).wait_send()
        line_copy(0, 0).wait_send()

    for turn in range(BLOCKS):
        out_copy(turn).wait_send()
        out_copy(turn, True).wait_recv()


ROWS = (7, 0, 1, 2, 3, 4, 5, 6)


def main_call(args):
    v = pltpu.VMEM
    packed_shape = (BLOCKS, NF, 2, YROWS, LEV)
    dma = pltpu.SemaphoreType.DMA
    scratch = [
        v((NF, 2 * XROWS, YROWS, LEV), bf16),
        v((NF, XROWS, YROWS, LEV), bf16),
        v((NF, XROWS, YROWS, LEV), bf16),
        v((NF, XROWS, YROWS, LEV), bf16),
        v((NF, BLOCKS, NODES, LEV), bf16),
        v((2, 2 * BLOCKS, NODES, LEV), f32),
        v((NF, YROWS, LEV), bf16),
        v((NF, YROWS, LEV), bf16),
        v((NF, YROWS, LEV), bf16),
        v((NF, YROWS, LEV), bf16),
        v((2, NF, 2 * XROWS, LEV), f32),
        v((2, 2, NF, XROWS, LEV), bf16),
        v((NF, XROWS, LEV), bf16),
        v((NF, XROWS, LEV), bf16),
        v((4, 16, LEV), f32),
        v((4, 16, LEV), f32),
        v((2, 16, LEV), f32),
        v((2, 16, LEV), f32),
        v((PAIRS, YROWS, 2 * LEV), f32),
        v((PAIRS, YROWS, 2 * LEV), f32),
        v((BLOCKS, 8, 4, 16), bf16),
        v((2 * BLOCKS, 8, 4, 16), bf16),
        v((1, 64), jnp.int32),
        v((NTEND, 4, 256), f32),
        v((LEV, LEV), f32),
        v((NTEND, LEV), f32),
        pltpu.SMEM((NTEND, NF), f32),
        v((2 * NODES, 2 * NODES), bf16),
        v((BLOCKS, NODES, NODES + 2 * XROWS), bf16),
        v((32, 256), f32),
        v((128, 16), f32),
        v((BLOCKS, CELLS, 128), bf16),
        v((2 * BLOCKS, 128, 128), bf16),
        v((256, 256), bf16),
    ]
    scratch += [v((128, 128), f32)] * 4
    scratch += [
        v((BLOCKS, NF, CELLS, LEV), f32),
        v((BLOCKS, NF, CELLS, 2 * LEV), bf16),
        v((BLOCKS, NF, CELLS, LEV), f32),
        v((BLOCKS, NF, CELLS, LEV), f32),
        v((BLOCKS, NTEND, CELLS, LEV), bf16),
        dma((9,)), dma((2 * BLOCKS,)), dma((BLOCKS,)), dma((BLOCKS,)),
        dma((9 + BLOCKS,)), dma((9 + BLOCKS,)), dma((4,)), dma((4,)),
        dma((3, CX * CY)), dma((2, CX * CY)), dma((BLOCKS,)), dma((BLOCKS,)),
    ]
    return pl.pallas_call(
        main_kernel,
        out_shape=(
            jax.ShapeDtypeStruct((2,) + packed_shape, bf16),
            jax.ShapeDtypeStruct(packed_shape, bf16),
            jax.ShapeDtypeStruct((2 * BLOCKS, 2 * YROWS, LEV), bf16),
            jax.ShapeDtypeStruct((NTEND, 128, LEV), bf16),
        ),
        in_specs=[HBM] * 10,
        out_specs=(VMEM,) * 4,
        scratch_shapes=scratch,
        compiler_params=pltpu.CompilerParams(
            collective_id=0, has_side_effects=True, vmem_limit_bytes=40 * 2**20
        ),
    )(*args)


def unpack_kernel(packed, landed, given, chosen, out, stage, sems):
    m = lax.axis_index("grp")

    def copy(k, block):
        rows = (m if k == 0 else 1 - m) * XROWS + 4 * block
        return pltpu.make_async_copy(
            stage.at[k, block], out.at[:, pl.ds(rows, 4)], sems.at[k, block]
        )

    for k in range(2):
        for block in range(BLOCKS):
            lines = given[(m if k == 0 else 1 - m) * BLOCKS + block]
            for f in range(NF):
                if f < NTEND:
                    added = mm(lines, chosen[f])
                for i in range(2):
                    line = packed[m, block, f, i] if k == 0 else landed[block, f, i]
                    line = line.astype(f32)
                    if f < NTEND:
                        line = line + added[i * YROWS:(i + 1) * YROWS]
                    stage[k, block, f, i] = line[:, :LEV // 2].astype(bf16)
                    moved = pltpu.roll(line, 64, 1)
                    stage[k, block, f, i + 2] = moved[:, :LEV // 2].astype(bf16)
            copy(k, block).start()
    for k in range(2):
        for block in range(BLOCKS):
            copy(k, block).wait()


def unpack_call(*arrays):
    return pl.pallas_call(
        unpack_kernel,
        out_shape=jax.ShapeDtypeStruct((NF, 2 * XROWS, YROWS, LEV // 2), bf16),
        in_specs=[VMEM] * 4,
        out_specs=HBM,
        scratch_shapes=[
            pltpu.VMEM((2, BLOCKS, NF, 4, YROWS, LEV // 2), bf16),
            pltpu.SemaphoreType.DMA((2, BLOCKS)),
        ],
        compiler_params=pltpu.CompilerParams(vmem_limit_bytes=24 * 2**20),
    )(*arrays)


def shards(
    section_levels, to_cells, to_nodes, owner_map, forcing, vertical_map, coupling, relaxation
):
    derive, advance = (jnp.asarray(c) for c in constants())
    operands = (
        section_levels, to_cells, jnp.swapaxes(to_nodes, 2, 3), owner_map.reshape(1, 64),
        forcing[0, 0], vertical_map, coupling, relaxation, derive, advance,
    )
    results = main_call([
        pltpu.with_memory_space_constraint(x, pltpu.HBM) for x in operands
    ])
    return unpack_call(*results)


def solution(mesh):
    in_specs = (
        P("grp", None, "gx", "gy", None),
        P("gx", "gy", None, None),
        P("gx", "gy", None, None),
        P("gx", "gy", None, None),
        P("gx", "gy", None, None, None),
        P(),
        P(),
        P(),
    )
    out_specs = P(None, "gx", "gy", "grp")
    return jax.shard_map(shards, mesh=mesh, in_specs=in_specs, out_specs=out_specs, check_vma=False)
```

time: 27.7 us -> 24.9 us (0.90)
  Pallas kernels: 27.6 us -> 24.8 us
    pallas_call x1, Pallas kernels: 26 us -> 23 us  [main_call(): pl.pallas_call(main_kernel, out_shape=(jax.ShapeDtypeStruct((2,) + packed...]
where the time goes in v4:
time: 24.9 us; the launch traced here: 24.8 us
  Pallas kernels  24.8 us (100%)
    pallas_call x1, Pallas kernels, main_call(): pl.pallas_call(main_kernel, out_shape=(jax.ShapeDtypeStruct((2,) + packed...  23 us
    pallas_call x1, Pallas kernels, unpack_call(): pl.pallas_call(unpack_kernel, out_shape=jax.ShapeDtypeStruct((NF, 2 * XRO...  1.83 us

profile of v4, /device:TPU:1, one launch (start us, length us, event | category | flops | bytes accessed | tf_op | source)
XLA Modules:
  0.0 24.8 jit_solution(7504133352724677052)
XLA Ops:
  0.0 23.0 %shard_map.100 = (bf16[2,4,10,2,32,128]{5,4,3,2,1,0:T(8,128)(2,1)S(1)}, bf16[4,10,2,32,128]{4,3,2,1,0:T(8,128)(2,1)S(1)}, bf16[8,64,128]{2,1,0:T(8,128)(2,1)S(1)}, bf16[8,128,128]{2,1,0:T(8,128)(2,1)S(1)}) custom-call(bf16[1,10,32,32,128]{4,3,2,1,0:T(8,128)(2,1)} %sec.1, bf16[8,8,4,16]{3,2,1,0:T(4,128)(2,1)} %tc.1, bf16[8,8,4,16]{3,2,1,0:T(4,128)(2,1)} %bitcast.3, ...), custom_call_target="tpu_custom_call" | custom-call | tf_op jit(solution)/shard_map/pallas_call | solution.py:572
  23.0 1.8 %shard_map.101 = bf16[10,32,32,64]{3,2,1,0:T(8,128)(2,1)} custom-call(bf16[2,4,10,2,32,128]{5,4,3,2,1,0:T(8,128)(2,1)S(1)} %get-tuple-element.9.packed, bf16[4,10,2,32,128]{4,3,2,1,0:T(8,128)(2,1)S(1)} %get-tuple-element.10.landed, bf16[8,64,128]{2,1,0:T(8,128)(2,1)S(1)} %get-tuple-element.11.given, bf16[8,128,128]{2,1,0:T(8,128)(2,1)S(1)} %get-tuple-element.12.chosen), custom_call_target="tpu_custom_call" | custom-call | tf_op jit(solution)/shard_map/pallas_call | solution.py:619

commit v5 on v4

--- a/solution.py
+++ b/solution.py
@@ -106,8 +106,8 @@
     def plane_peer(j):
         return (1, z * CX + (x + j // CY) % CX, (gy + j % CY) % CY)
 
-    def line_peer(member, j):
-        return (member, ((z + j) % CZ) * CX + x, gy)
+    def line_peer(j):
+        return (1, ((z + j) % CZ) * CX + x, gy)
 
     barrier = pltpu.get_barrier_semaphore()
 
@@ -193,15 +193,19 @@
             f_send.at[0, j], f_recv.at[0, j], device_id=plane_peer(j), device_id_type=MESH,
         )
 
-    def line_copy(member, j, arriving=False):
+    def line_copy(j, arriving=False):
         to, me = (z + j) % CZ, z
         if arriving:
             me = (z + CZ - j) % CZ
         return pltpu.make_async_remote_copy(
             fs2.at[pl.ds(pl.multiple_of(to * 16, 16), 16)],
             fb2.at[pl.ds(pl.multiple_of(me * 16, 16), 16)],
-            f_send.at[1 + member, j], f_recv.at[1, j],
-            device_id=line_peer(member, j), device_id_type=MESH,
+            f_send.at[1, j], f_recv.at[1, j], device_id=line_peer(j), device_id_type=MESH,
+        )
+
+    def table_copy():
+        return pltpu.make_async_remote_copy(
+            fb2, fb2, f_send.at[1, 0], f_recv.at[1, 0], device_id=partner, device_id_type=MESH
         )
 
     @pl.when(m == 0)
@@ -211,7 +215,6 @@
             current_in(block).start()
         greet([partner, (0, gx, down), (0, gx, up)])
         greet([(1, left, gy), (1, left, down), (1, left, up)])
-        greet([line_peer(1, j) for j in range(1, CZ)])
         for k, copy in enumerate(small):
             if k != 1:
                 copy.start()
@@ -279,10 +282,10 @@
     @pl.when(m == 1)
     def _():
         small[0].start()
+        greet([plane_peer(j) for j in PLANE])
+        greet([line_peer(j) for j in LINE])
+        greet([(1, right, gy), (1, right, down), (1, right, up)])
         greet([partner, (0, gx, down), (0, gx, up)])
-        greet([(1, right, gy), (1, right, down), (1, right, up)])
-        greet([plane_peer(j) for j in range(1, CX * CY)])
-        greet([line_peer(1, j) for j in range(1, CZ)])
         for turn in range(BLOCKS):
             start_in(turn).start()
         for copy in small[1:]:
@@ -305,11 +308,15 @@
         fa[...] = total
         xlo[...] = jnp.zeros_like(xlo)
         clo[...] = jnp.zeros_like(clo)
-        pl.semaphore_wait(barrier, 36)
-        for j in range(1, CX * CY):
+        pl.semaphore_wait(barrier, 29)
+        for j in PLANE:
             plane_copy(j, False).start()
         for turn in range(BLOCKS):
             start_out(turn).start()
+        for copy in edge_copies((0, 1, 2)):
+            copy.wait_recv()
+        for copy in edge_copies((7, 8)) + corner_copies():
+            copy.start()
         mine = pl.ds(pl.multiple_of((x * CY + gy) * 8, 8), 8)
         fb1[mine, :] = fa[mine, :]
 
@@ -318,14 +325,9 @@
             plane_copy(j, True).wait_recv()
         for k in range(CZ):
             fs2[16 * k:16 * k + 16, :] = fb1[pl.ds(k, 16, stride=CZ), :]
-        for j in range(1, CZ):
-            for member in range(2):
-                line_copy(member, j).start()
+        for j in LINE:
+            line_copy(j).start()
         mine = pl.ds(pl.multiple_of(z * 16, 16), 16)
-        pltpu.make_async_remote_copy(
-            fs2.at[mine], fb2.at[mine], f_send.at[1, 0], f_recv.at[1, 0],
-            device_id=partner, device_id_type=MESH,
-        ).start()
         fb2[mine, :] = fs2[mine, :]
 
     for copy in small[3:]:
@@ -376,10 +378,6 @@
     def _():
         small[1].wait()
         small[2].wait()
-        for copy in edge_copies((0, 1, 2)):
-            copy.wait_recv()
-        for copy in edge_copies((7, 8)) + corner_copies():
-            copy.start()
         relay()
         for copy in edge_copies((4, 6)):
             copy.wait_recv()
@@ -471,13 +469,13 @@
 
     @pl.when(m == 0)
     def _():
-        for j in range(CZ):
-            line_copy(0, j, True).wait_recv()
+        table_copy().wait_recv()
 
     @pl.when(m == 1)
     def _():
         for j in range(1, CZ):
-            line_copy(1, j, True).wait_recv()
+            line_copy(j, True).wait_recv()
+        table_copy().start()
 
     table = fb2[...]
     lines = mm2(from0, table) + mm2(from1, pltpu.roll(table, 96, 1))
@@ -506,9 +504,8 @@
         for j in range(1, CX * CY):
             plane_copy(j, False).wait_send()
         for j in range(1, CZ):
-            for member in range(2):
-                line_copy(member, j).wait_send()
-        line_copy(0, 0).wait_send()
+            line_copy(j).wait_send()
+        table_copy().wait_send()
 
     for turn in range(BLOCKS):
         out_copy(turn).wait_send()
@@ -516,6 +513,14 @@
 
 
 ROWS = (7, 0, 1, 2, 3, 4, 5, 6)
+
+
+def hops_to(j, count):
+    return min(j % count, count - j % count)
+
+
+PLANE = sorted(range(1, CX * CY), key=lambda j: -hops_to(j // CY, CX) - hops_to(j, CY))
+LINE = sorted(range(1, CZ), key=lambda j: -hops_to(j, CZ))
 
 
 def main_call(args):
@@ -567,7 +572,7 @@
         v((BLOCKS, NTEND, CELLS, LEV), bf16),
         dma((9,)), dma((2 * BLOCKS,)), dma((BLOCKS,)), dma((BLOCKS,)),
         dma((9 + BLOCKS,)), dma((9 + BLOCKS,)), dma((4,)), dma((4,)),
-        dma((3, CX * CY)), dma((2, CX * CY)), dma((BLOCKS,)), dma((BLOCKS,)),
+        dma((2, CX * CY)), dma((2, CX * CY)), dma((BLOCKS,)), dma((BLOCKS,)),
     ]
     return pl.pallas_call(
         main_kernel,

time: 24.9 us -> 23.9 us (0.960)
  Pallas kernels: 24.8 us -> 23.9 us
    pallas_call x1, Pallas kernels: 23 us -> 22 us  [main_call(): pl.pallas_call(main_kernel, out_shape=(jax.ShapeDtypeStruct((2,) + packed...]
where the time goes in v5:
time: 23.9 us
  Pallas kernels  23.9 us (100%)
    pallas_call x1, Pallas kernels, main_call(): pl.pallas_call(main_kernel, out_shape=(jax.ShapeDtypeStruct((2,) + packed...  22 us
    pallas_call x1, Pallas kernels, unpack_call(): pl.pallas_call(unpack_kernel, out_shape=jax.ShapeDtypeStruct((NF, 2 * XRO...  1.83 us

profile of v5, /device:TPU:1, one launch (start us, length us, event | category | flops | bytes accessed | tf_op | source)
XLA Modules:
  0.0 23.9 jit_solution(18139135148717878336)
XLA Ops:
  0.0 22.0 %shard_map.100 = (bf16[2,4,10,2,32,128]{5,4,3,2,1,0:T(8,128)(2,1)S(1)}, bf16[4,10,2,32,128]{4,3,2,1,0:T(8,128)(2,1)S(1)}, bf16[8,64,128]{2,1,0:T(8,128)(2,1)S(1)}, bf16[8,128,128]{2,1,0:T(8,128)(2,1)S(1)}) custom-call(bf16[1,10,32,32,128]{4,3,2,1,0:T(8,128)(2,1)} %sec.1, bf16[8,8,4,16]{3,2,1,0:T(4,128)(2,1)} %tc.1, bf16[8,8,4,16]{3,2,1,0:T(4,128)(2,1)} %bitcast.3, ...), custom_call_target="tpu_custom_call" | custom-call | tf_op jit(solution)/shard_map/pallas_call | solution.py:577
  22.0 1.8 %shard_map.101 = bf16[10,32,32,64]{3,2,1,0:T(8,128)(2,1)} custom-call(bf16[2,4,10,2,32,128]{5,4,3,2,1,0:T(8,128)(2,1)S(1)} %get-tuple-element.9.packed, bf16[4,10,2,32,128]{4,3,2,1,0:T(8,128)(2,1)S(1)} %get-tuple-element.10.landed, bf16[8,64,128]{2,1,0:T(8,128)(2,1)S(1)} %get-tuple-element.11.given, bf16[8,128,128]{2,1,0:T(8,128)(2,1)S(1)} %get-tuple-element.12.chosen), custom_call_target="tpu_custom_call" | custom-call | tf_op jit(solution)/shard_map/pallas_call | solution.py:624

commit v6 on v5

--- a/solution.py
+++ b/solution.py
@@ -469,6 +469,22 @@
 
     @pl.when(m == 0)
     def _():
+        for copy in edge_copies((0, 1, 2, 3, 4, 5, 6, 9, 10, 11, 12)):
+            copy.wait_send()
+
+    @pl.when(m == 1)
+    def _():
+        for turn in range(BLOCKS):
+            start_out(turn).wait_send()
+        for copy in edge_copies((7, 8)) + corner_copies():
+            copy.wait_send()
+        for j in range(1, CX * CY):
+            plane_copy(j, False).wait_send()
+        for j in range(1, CZ):
+            line_copy(j).wait_send()
+
+    @pl.when(m == 0)
+    def _():
         table_copy().wait_recv()
 
     @pl.when(m == 1)
@@ -490,21 +506,8 @@
         high = both.astype(bf16).astype(f32)
         given[block] = jnp.where(quarter % 2 == 0, high, both - high).astype(bf16)
 
-    @pl.when(m == 0)
-    def _():
-        for copy in edge_copies((0, 1, 2, 3, 4, 5, 6, 9, 10, 11, 12)):
-            copy.wait_send()
-
     @pl.when(m == 1)
     def _():
-        for turn in range(BLOCKS):
-            start_out(turn).wait_send()
-        for copy in edge_copies((7, 8)) + corner_copies():
-            copy.wait_send()
-        for j in range(1, CX * CY):
-            plane_copy(j, False).wait_send()
-        for j in range(1, CZ):
-            line_copy(j).wait_send()
         table_copy().wait_send()
 
     for turn in range(BLOCKS):

time: 23.9 us -> 23.9 us (level)
  no operation moved by 1% of the time
where the time goes in v6:
time: 23.9 us
  Pallas kernels  23.9 us (100%)
    pallas_call x1, Pallas kernels, main_call(): pl.pallas_call(main_kernel, out_shape=(jax.ShapeDtypeStruct((2,) + packed...  22 us
    pallas_call x1, Pallas kernels, unpack_call(): pl.pallas_call(unpack_kernel, out_shape=jax.ShapeDtypeStruct((NF, 2 * XRO...  1.83 us

profile of v6, /device:TPU:1, one launch (start us, length us, event | category | flops | bytes accessed | tf_op | source)
XLA Modules:
  0.0 23.9 jit_solution(6771842682780399927)
XLA Ops:
  0.0 22.0 %shard_map.100 = (bf16[2,4,10,2,32,128]{5,4,3,2,1,0:T(8,128)(2,1)S(1)}, bf16[4,10,2,32,128]{4,3,2,1,0:T(8,128)(2,1)S(1)}, bf16[8,64,128]{2,1,0:T(8,128)(2,1)S(1)}, bf16[8,128,128]{2,1,0:T(8,128)(2,1)S(1)}) custom-call(bf16[1,10,32,32,128]{4,3,2,1,0:T(8,128)(2,1)} %sec.1, bf16[8,8,4,16]{3,2,1,0:T(4,128)(2,1)} %tc.1, bf16[8,8,4,16]{3,2,1,0:T(4,128)(2,1)} %bitcast.3, ...), custom_call_target="tpu_custom_call" | custom-call | tf_op jit(solution)/shard_map/pallas_call | solution.py:580
  22.0 1.8 %shard_map.101 = bf16[10,32,32,64]{3,2,1,0:T(8,128)(2,1)} custom-call(bf16[2,4,10,2,32,128]{5,4,3,2,1,0:T(8,128)(2,1)S(1)} %get-tuple-element.9.packed, bf16[4,10,2,32,128]{4,3,2,1,0:T(8,128)(2,1)S(1)} %get-tuple-element.10.landed, bf16[8,64,128]{2,1,0:T(8,128)(2,1)S(1)} %get-tuple-element.11.given, bf16[8,128,128]{2,1,0:T(8,128)(2,1)S(1)} %get-tuple-element.12.chosen), custom_call_target="tpu_custom_call" | custom-call | tf_op jit(solution)/shard_map/pallas_call | solution.py:627
